TPU v7x, 256 devices: a whole 4x4x8 slice. The times are simulated.
256 devices in a mesh: row: 16 (over z_hi, y, core), col: 16 (over z_lo, x).
Axes of the slice: x: 4, y: 4, z: 8 (z_hi: 2, z_lo: 4; z = z_hi * 4 + z_lo), core: 2. Of those that a mesh axis runs over, the one named last changes fastest.
Arguments:
- activations: bfloat16 [4, 2048, 5120], P(None, None, 'row'), may hold values from -6 to 6
- out_grads: bfloat16 [4, 2048, 13824], P(None, 'row', 'col'), may hold values from -6 to 6
- hash_seeds: int32 [2], replicated, may hold values from 0 to 1073741823
- offsets: int32 [2], replicated, may hold values from 0 to 1048575
Outputs:
- features: float32 [4, 32, 64], P(None, 'col', 'row')
All inputs are finite; a program needn't handle non-finite values.
Results may differ from a plain program's by a relative error of at most 0.0041.
Values sent between devices are 32-bit elements; how exact they have to be, the bound alone decides.
No kernel may reach another device: no remote copies, remote signals or barrier semaphores. Data moves between devices by JAX's collectives and lax.ppermute only.
A program may use at most 64 MiB of HBM per device.

v0:
```python
import math

import jax
import jax.numpy as jnp
from jax import lax
from jax.sharding import PartitionSpec as P

D = 5120
FF = 13824
K_IN = 32
K_OUT = 64
SEQ_LEN = 2048


def scramble(counter, seed_value):
    hashed = jnp.bitwise_xor(counter, seed_value)
    shift_by = jnp.full_like(hashed, 16)
    hashed = hashed * jnp.int32(73244475)
    hashed = jnp.bitwise_xor(hashed, lax.shift_right_logical(hashed, shift_by))
    hashed = hashed * jnp.int32(73244475)
    hashed = jnp.bitwise_xor(hashed, lax.shift_right_logical(hashed, shift_by))
    return hashed


def unit_draw(hashed):
    top_bits = lax.shift_right_logical(hashed, jnp.full_like(hashed, 8))
    return (top_bits.astype(jnp.float32) + 0.5) * (1.0 / 16777216.0)


def normal_table(seed_value, offset, first_row, row_count, first_col, col_count, stride, fan_in):
    row_ids = first_row + lax.broadcasted_iota(jnp.int32, (row_count, col_count), 0)
    col_ids = first_col + lax.broadcasted_iota(jnp.int32, (row_count, col_count), 1)
    counter = offset + row_ids * stride + col_ids
    radius = jnp.sqrt(-2.0 * jnp.log(unit_draw(scramble(2 * counter, seed_value))))
    angle_part = unit_draw(scramble(2 * counter + 1, seed_value))
    normal_values = radius * jnp.cos(2.0 * math.pi * angle_part) * fan_in ** (-0.5)
    return normal_values.astype(jnp.bfloat16)


def body(activations, out_grads, hash_seeds, offsets):
    row_index = lax.axis_index("row")
    col_index = lax.axis_index("col")
    rows_here = activations.shape[2]
    cols_here = out_grads.shape[2]
    positions = out_grads.shape[1]
    factor_here = K_IN // lax.axis_size("col")
    norm_factor = SEQ_LEN ** (-0.5)
    in_table = normal_table(
        hash_seeds[0],
        offsets[0],
        row_index * rows_here,
        rows_here,
        col_index * factor_here,
        factor_here,
        K_IN,
        D,
    )
    out_table = normal_table(
        hash_seeds[1], offsets[1], col_index * cols_here, cols_here, 0, K_OUT, K_OUT, FF
    )
    input_terms = jnp.einsum(
        "spd,dk->spk", activations, in_table, preferred_element_type=jnp.float32
    )
    output_terms = jnp.einsum(
        "spf,fk->spk", out_grads, out_table, preferred_element_type=jnp.float32
    )
    input_whole = lax.psum(input_terms, "row")
    input_side = lax.dynamic_slice_in_dim(input_whole, row_index * positions, positions, 1)
    output_side = lax.psum(output_terms, "col")
    partial_features = (
        jnp.einsum("spi,spj->sij", input_side, output_side, precision=lax.Precision.HIGHEST)
        * norm_factor
    )
    return lax.psum_scatter(partial_features, "row", scatter_dimension=2, tiled=True)


def solution(mesh):
    return jax.shard_map(
        body,
        mesh=mesh,
        in_specs=(P(None, None, "row"), P(None, "row", "col"), P(), P()),
        out_specs=P(None, "col", "row"),
        check_vma=False,
    )
```

profile of v0, /device:TPU:1, one launch (start us, length us, event | category | flops | bytes accessed | tf_op | source)
XLA Modules:
  0.0 396.7 jit_solution(4162277089788032171)
XLA Ops:
  6.5 0.0 copy-start
  6.5 0.0 copy-start.1
  6.5 0.0 all-reduce.4.cloned.1.call-start
  6.5 1.4 fusion.84
  7.9 1.4 fusion.83
  9.3 0.6 multiply_add_fusion.1
  9.9 4.6 %convolution_bitcast_fusion = f32[4,2048,2]{1,2,0:T(2,128)} fusion(bf16[4,2048,320]{1,2,0:T(8,128)(2,1)} %param.4, s32[]{:T(128)} %bitcast.1, s32[320]{0:T(512)S(1)} %multiply_add_fusion.1, s32[2]{0:T(128)S(1)} %iota_add_fusion), kind=kOutput, calls=%fused_computation | convolution fusion | flops 10504320 | bytes 5309708 | tf_op jit(solution)/shard_map/spd,dk->spk/dot_general | solution.py:61
  14.5 0.0 all-reduce.4.cloned.1.call-update
  14.6 0.0 all-reduce.6.cloned.1.call-start
  14.6 0.6 multiply_add_fusion
  15.3 0.0 copy-done
  15.3 2.4 convolution_bitcast_fusion.1
  17.7 0.0 all-reduce.6.cloned.1.call-update
  17.7 0.0 copy-done.1
  17.8 0.6 dynamic-slice
  19.0 163.9 %all-reduce.4.cloned.1.call-done = f32[4,2048,2]{1,2,0:T(2,128)} async-done(((f32[4,2048,2]{1,2,0:T(2,128)}), f32[4,2048,2]{1,2,0:T(2,128)}) %all-reduce.4.cloned.1.call-update) | async-done | bytes 65552 | tf_op jit(solution)/shard_map/psum | solution.py:67
  182.9 152.3 %all-reduce.6.cloned.1.call-done = f32[4,128,64]{1,2,0:T(8,128)} async-done(((f32[4,128,64]{1,2,0:T(8,128)}), f32[4,128,64]{1,2,0:T(8,128)}) %all-reduce.6.cloned.1.call-update) | async-done | bytes 131088 | tf_op jit(solution)/shard_map/psum | solution.py:69
  335.2 1.2 convolution_multiply_fusion
  336.4 52.8 %all-reduce = f32[4,2,64]{2,1,0:T(2,128)S(1)} all-reduce(f32[4,2,64]{2,1,0:T(2,128)S(1)} %convolution_multiply_fusion), channel_id=2, replica_groups=mesh['row'=16,'col'=16] {'row'}, use_global_device_ids=true, to_apply=%region_2.0.clone | all-reduce | flops 512 | bytes 4096
  389.1 0.7 constant_dynamic-slice_fusion
  (1 shorter events, 0.0 us)
Async XLA Ops:
  6.5 8.7 %copy-start = (bf16[4,128,864]{1,2,0:T(8,128)(2,1)S(1)}, bf16[4,128,864]{1,2,0:T(8,128)(2,1)}, u32[]{:S(2)}) copy-start(bf16[4,128,864]{1,2,0:T(8,128)(2,1)} %param.5) | copy-start | bytes 2654212
  6.5 11.2 %copy-start.1 = (u32[256]{0:T(256)S(1)}, u32[256]{0:T(256)}, u32[]{:S(2)}) copy-start(u32[256]{0:T(256)} %constant.18) | copy-start | bytes 3076
  6.5 176.4 %all-reduce.4.cloned.1.call-start = ((), (), s32[]{:S(2)}) async-start(), calls=%async_computation | async-start | bytes 131072 | tf_op jit(solution)/shard_map/psum | solution.py:67
  14.6 320.6 %all-reduce.6.cloned.1.call-start = ((), (), s32[]{:S(2)}) async-start(), calls=%async_computation.1 | async-start | bytes 262144 | tf_op jit(solution)/shard_map/psum | solution.py:69
Sparse Core Ops, SparseCore 0:
  14.7 168.1 all-reduce.3
  185.7 149.4 all-reduce.5
where the time goes:
time: 397 us
  waiting for transfers between devices  316 us (80%)
  blocking collectives  52.8 us (13%)
  between operations  14.1 us (4%)
  matrix products  8.3 us (2%)
  local copies, waits for them, and re-layouts  3.99 us (1%)
    psum x1, waiting for transfers between devices, body(): input_whole = lax.psum(input_terms, 'row')  164 us
    psum x1, waiting for transfers between devices, body(): output_side = lax.psum(output_terms, 'col')  152 us
    unnamed x1, blocking collectives  52.8 us
  transfers between devices with their start and end apart: 2, of which 2 were waited for; matrix products, arithmetic and copies ran while one was open for 1% of the time, Pallas kernels for 0%

commit v1 on v0

v1 whole, which is shorter than its diff:
```python
import functools

import jax
import jax.numpy as jnp
from jax import lax
from jax.experimental import pallas as pl
from jax.experimental.pallas import tpu as pltpu
from jax.sharding import PartitionSpec as P

D = 5120
FF = 13824
K_IN = 32
K_OUT = 64
SEQ_LEN = 2048
SEQS = 4
ROWS = 16
COLS = 16
LANES = 128
MULTIPLIER = 73244475
VMEM_LIMIT = 60 * 1024 * 1024

SIN_TURN = (
    6.283185280154403,
    -41.34168061334532,
    81.60247636883796,
    -76.5811726421402,
    39.75982706857711,
)


def scramble(counter, seed_value):
    hashed = counter ^ seed_value
    hashed = hashed * jnp.int32(MULTIPLIER)
    hashed = hashed ^ lax.shift_right_logical(hashed, jnp.full_like(hashed, 16))
    hashed = hashed * jnp.int32(MULTIPLIER)
    return hashed ^ lax.shift_right_logical(hashed, jnp.full_like(hashed, 16))


def unit_draw(hashed):
    top_bits = lax.shift_right_logical(hashed, jnp.full_like(hashed, 8))
    return (top_bits.astype(jnp.float32) + 0.5) * (1.0 / 16777216.0)


def cos_turn(angle):
    quarter = jnp.abs(angle - 0.5) - 0.25
    square = quarter * quarter
    total = jnp.full_like(square, SIN_TURN[-1])
    for term in SIN_TURN[-2::-1]:
        total = total * square + term
    return total * quarter


def normal_draw(counter, seed_value, fan_in):
    radius = jnp.sqrt(-2.0 * jnp.log(unit_draw(scramble(2 * counter, seed_value))))
    angle = unit_draw(scramble(2 * counter + 1, seed_value))
    return (radius * cos_turn(angle) * fan_in ** (-0.5)).astype(jnp.bfloat16)


def input_kernel(seeds, offsets, acts, terms, held, arrived):
    row = lax.axis_index("row")
    seq = lax.rem(lax.axis_index("col"), SEQS)
    here = acts.shape[1]
    fetch = pltpu.make_async_copy(acts.at[seq], held, arrived)
    fetch.start()
    shape = (K_IN, here)
    slot = lax.broadcasted_iota(jnp.int32, shape, 0)
    feature = row * here + lax.broadcasted_iota(jnp.int32, shape, 1)
    factor = (slot & 15) * 2 + lax.shift_right_logical(slot, jnp.full_like(slot, 4))
    table = normal_draw(offsets[0] + feature * K_IN + factor, seeds[0], D)
    fetch.wait()
    for part in range(4):
        product = jnp.dot(
            table, held[:, part * 512 : (part + 1) * 512], preferred_element_type=jnp.float32
        )
        for piece in range(4):
            terms[part * 4 + piece] = product[:, piece * LANES : (piece + 1) * LANES]


def output_kernel(seeds, offsets, grads, own, near, far, both, held, arrived):
    col = lax.axis_index("col")
    seq = lax.rem(col, SEQS)
    here = grads.shape[1]
    fetches = []
    for m in range(SEQS):
        fetch = pltpu.make_async_copy(grads.at[seq ^ m], held.at[m], arrived.at[m])
        fetch.start()
        fetches.append(fetch)
    shape = (K_OUT, here)
    factor = lax.broadcasted_iota(jnp.int32, shape, 0)
    feature = col * here + lax.broadcasted_iota(jnp.int32, shape, 1)
    table = normal_draw(offsets[1] + feature * K_OUT + factor, seeds[1], FF)
    for m, out in ((3, both), (2, far), (1, near), (0, own)):
        fetches[m].wait()
        out[...] = jnp.dot(table, held[m], preferred_element_type=jnp.float32)


def feature_kernel(terms, own, near, far, both, spread):
    side_in = terms[0]
    for r in range(1, ROWS):
        side_in = side_in + terms[r]
    side_out = (own[...] + near[...]) + (far[...] + both[...])
    halves = [
        lax.dot_general(
            side_in[b * 16 : (b + 1) * 16],
            side_out,
            (((1,), (1,)), ((), ())),
            precision=lax.Precision.HIGHEST,
            preferred_element_type=jnp.float32,
        )
        for b in range(2)
    ]
    paired = jnp.concatenate(halves, axis=1) * SEQ_LEN ** (-0.5)
    for r in range(ROWS):
        shifted = paired if r == 0 else pltpu.roll(paired, LANES - 4 * r, 1)
        spread[r * COLS : (r + 1) * COLS] = shifted


def body(activations, out_grads, hash_seeds, offsets):
    acts = jnp.swapaxes(activations, 1, 2)
    grads = jnp.swapaxes(out_grads, 1, 2)
    here_in = acts.shape[1]
    here_out = grads.shape[1]
    smem = pl.BlockSpec(memory_space=pltpu.SMEM)
    vmem = pl.BlockSpec(memory_space=pltpu.VMEM)
    anywhere = pl.BlockSpec(memory_space=pl.ANY)
    params = pltpu.CompilerParams(vmem_limit_bytes=VMEM_LIMIT)

    side = jax.ShapeDtypeStruct((K_OUT, LANES), jnp.float32)
    own, near, far, both = pl.pallas_call(
        output_kernel,
        out_shape=[side] * 4,
        in_specs=[smem, smem, anywhere],
        out_specs=[vmem] * 4,
        scratch_shapes=[
            pltpu.VMEM((SEQS, here_out, LANES), jnp.bfloat16),
            pltpu.SemaphoreType.DMA((SEQS,)),
        ],
        compiler_params=params,
        name="output_terms",
    )(hash_seeds, offsets, grads)
    terms = pl.pallas_call(
        input_kernel,
        out_shape=jax.ShapeDtypeStruct((ROWS, K_IN, LANES), jnp.float32),
        in_specs=[smem, smem, anywhere],
        out_specs=vmem,
        scratch_shapes=[
            pltpu.VMEM((here_in, SEQ_LEN), jnp.bfloat16),
            pltpu.SemaphoreType.DMA,
        ],
        compiler_params=params,
        name="input_terms",
    )(hash_seeds, offsets, acts)

    def across(value, distance):
        return lax.ppermute(value, "col", [(c, c ^ distance) for c in range(COLS)])

    near, far, both = across(near, 1), across(far, 2), across(both, 3)
    terms = lax.all_to_all(terms, "row", 0, 0, tiled=True)
    spread = pl.pallas_call(
        feature_kernel,
        out_shape=jax.ShapeDtypeStruct((ROWS * COLS, LANES), jnp.float32),
        in_specs=[vmem] * 5,
        out_specs=vmem,
        compiler_params=params,
        name="feature_partials",
    )(terms, own, near, far, both)
    spread = lax.all_to_all(spread, ("row", "col"), 0, 0, tiled=True)
    summed = jnp.sum(spread.reshape(ROWS * COLS // SEQS, SEQS, LANES), axis=0)
    return summed.reshape(SEQS, 2, K_OUT)[:, :, :4]


def solution(mesh):
    return jax.shard_map(
        body,
        mesh=mesh,
        in_specs=(P(None, None, "row"), P(None, "row", "col"), P(), P()),
        out_specs=P(None, "col", "row"),
        check_vma=False,
    )
```

time: 397 us -> 55.5 us (0.14)
  waiting for transfers between devices: 316 us -> 4.28 us
  blocking collectives: 52.8 us -> 24.5 us
  starting transfers between devices: 0.04 us -> 16.6 us
  between operations: 14.1 us -> 0.04 us
  Pallas kernels: 0 us -> 8.38 us
  matrix products: 8.3 us -> 0 us
    psum x2 -> x0, waiting for transfers between devices: 316 us -> none  [the longest x1 164 us: body(): input_whole = lax.psum(input_terms, 'row')]
    unnamed x1 -> x0, blocking collectives: 52.8 us -> none
    all_to_all x0 -> x1, blocking collectives: none -> 24.5 us  [body(): spread = lax.all_to_all(spread, ('row', 'col'), 0, 0, tiled=True)]
    all_to_all x0 -> x1, starting transfers between devices: none -> 12.6 us  [body(): terms = lax.all_to_all(terms, 'row', 0, 0, tiled=True)]
    pallas_call x0 -> x3, Pallas kernels: none -> 8.38 us  [the longest x1 3.3 us: body(): pl.pallas_call(output_kernel, out_shape=[side] * 4, in_specs=[smem, smem,...]
    dot_general x3 -> x0, matrix products: 8.3 us -> none  [the longest x1 4.65 us: body(): jnp.einsum('spd,dk->spk', activations, in_table, preferred_element_type=j...]
    ppermute x0 -> x3, waiting for transfers between devices: none -> 4.28 us  [across(): return lax.ppermute(value, 'col', [(c, c ^ distance) for c in range(COLS)])]
  transfers between devices with their start and end apart: 2 -> 4, of which waited for: 2 -> 2; matrix products, arithmetic and copies ran while one was open for 1% -> 0% of each run, Pallas kernels for 0% -> 6%
where the time goes in v1:
time: 55.5 us; the launch traced here: 55.2 us
  blocking collectives  24.5 us (44%)
  starting transfers between devices  16.6 us (30%)
  Pallas kernels  8.38 us (15%)
  waiting for transfers between devices  4.28 us (8%)
  local copies, waits for them, and re-layouts  1.38 us (2%)
    all_to_all x1, blocking collectives, body(): spread = lax.all_to_all(spread, ('row', 'col'), 0, 0, tiled=True)  24.5 us
    all_to_all x1, starting transfers between devices, body(): terms = lax.all_to_all(terms, 'row', 0, 0, tiled=True)  12.6 us
    ppermute x3, waiting for transfers between devices, across(): return lax.ppermute(value, 'col', [(c, c ^ distance) for c in range(COLS)])  4.28 us
    ppermute x3, starting transfers between devices, across(): return lax.ppermute(value, 'col', [(c, c ^ distance) for c in range(COLS)])  3.97 us
    pallas_call x1, Pallas kernels, body(): pl.pallas_call(output_kernel, out_shape=[side] * 4, in_specs=[smem, smem,...  3.3 us
    pallas_call x1, Pallas kernels, body(): pl.pallas_call(input_kernel, out_shape=jax.ShapeDtypeStruct((ROWS, K_IN,...  3.04 us
    pallas_call x1, Pallas kernels, body(): pl.pallas_call(feature_kernel, out_shape=jax.ShapeDtypeStruct((ROWS * COL...  2.04 us
  transfers between devices with their start and end apart: 4, of which 2 were waited for; matrix products, arithmetic and copies ran while one was open for 0% of the time, Pallas kernels for 6%

profile of v1, /device:TPU:1, one launch (start us, length us, event | category | flops | bytes accessed | tf_op | source)
XLA Modules:
  0.0 55.2 jit_solution(5116470017680616824)
XLA Ops:
  0.0 3.0 %input_terms.1 = f32[16,32,128]{2,1,0:T(8,128)} custom-call(s32[2]{0:T(128)} %seeds.3, s32[2]{0:T(128)} %offsets.3, bf16[4,320,2048]{2,1,0:T(8,128)(2,1)} %bitcast.7), custom_call_target="tpu_custom_call" | custom-call | tf_op jit(solution)/shard_map/input_terms/pallas_call | solution.py:141
  3.0 12.6 %all-to-all-start = ((f32[16,32,128]{2,1,0:T(8,128)}), f32[16,32,128]{2,1,0:T(8,128)S(1)}, u32[]{:S(2)}, u32[]{:S(2)}) async-start(f32[16,32,128]{2,1,0:T(8,128)} %input_terms.1), calls=%async_computation | async-start | bytes 524288 | tf_op jit(solution)/shard_map/all_to_all | solution.py:158
  15.7 3.3 %output_terms.1 = (f32[64,128]{1,0:T(8,128)}, f32[64,128]{1,0:T(8,128)}, f32[64,128]{1,0:T(8,128)}, f32[64,128]{1,0:T(8,128)}) custom-call(s32[2]{0:T(128)} %seeds.3, s32[2]{0:T(128)} %offsets.3, bf16[4,864,128]{2,1,0:T(8,128)(2,1)} %bitcast.8), custom_call_target="tpu_custom_call" | custom-call | tf_op jit(solution)/shard_map/output_terms/pallas_call | solution.py:129
  19.0 1.3 %collective-permute-start = (f32[64,128]{1,0:T(8,128)}, f32[64,128]{1,0:T(8,128)S(1)}, u32[]{:S(2)}, u32[]{:S(2)}) collective-permute-start(f32[64,128]{1,0:T(8,128)} %get-tuple-element.10), channel_id=1, source_target_pairs={{0,1},{1,0},{2,3},{3,2},{4,5},{5,4},{6,7},{7,6},{8,9},{9,8},{10,11... | collective-permute-start | bytes 98312 | tf_op jit(solution)/shard_map/ppermute | solution.py:155
  20.3 2.5 %collective-permute-start.1 = (f32[64,128]{1,0:T(8,128)}, f32[64,128]{1,0:T(8,128)S(1)}, u32[]{:S(2)}, u32[]{:S(2)}) collective-permute-start(f32[64,128]{1,0:T(8,128)} %get-tuple-element.11), channel_id=1, source_target_pairs={{0,2},{1,3},{2,0},{3,1},{4,6},{5,7},{6,4},{7,5},{8,10},{9,11},{10,... | collective-permute-start | bytes 98312 | tf_op jit(solution)/shard_map/ppermute | solution.py:155
  22.7 0.2 collective-permute-start.2
  22.9 0.0 collective-permute-done.near
  22.9 0.0 copy-start.1
  23.0 2.4 %collective-permute-done.1.far = f32[64,128]{1,0:T(8,128)S(1)} collective-permute-done((f32[64,128]{1,0:T(8,128)}, f32[64,128]{1,0:T(8,128)S(1)}, u32[]{:S(2)}, u32[]{:S(2)}) %collective-permute-start.1) | collective-permute-done | bytes 32800 | tf_op jit(solution)/shard_map/ppermute | solution.py:155
  25.4 0.0 copy-start.2
  25.4 1.8 %collective-permute-done.2.both = f32[64,128]{1,0:T(8,128)S(1)} collective-permute-done((f32[64,128]{1,0:T(8,128)}, f32[64,128]{1,0:T(8,128)S(1)}, u32[]{:S(2)}, u32[]{:S(2)}) %collective-permute-start.2) | collective-permute-done | bytes 32800 | tf_op jit(solution)/shard_map/ppermute | solution.py:155
  27.2 0.0 copy-start.3
  27.2 0.0 all-to-all-done.terms
  27.2 0.0 copy-start
  27.2 0.0 copy-done.1
  27.2 0.0 copy-done.2
  27.3 0.6 %copy-done.3 = f32[64,128]{1,0:T(8,128)} copy-done((f32[64,128]{1,0:T(8,128)}, f32[64,128]{1,0:T(8,128)S(1)}, u32[]{:S(2)}) %copy-start.3) | copy-done | bytes 32792
  27.8 0.1 copy-done
  27.9 2.0 %feature_partials.1 = f32[256,128]{1,0:T(8,128)} custom-call(f32[16,32,128]{2,1,0:T(8,128)} %copy-done, f32[64,128]{1,0:T(8,128)} %get-tuple-element.9.own, f32[64,128]{1,0:T(8,128)} %copy-done.1, f32[64,128]{1,0:T(8,128)} %copy-done.2, f32[64,128]{1,0:T(8,128)} %copy-done.3), custom_call_target="tpu_custom_call" | custom-call | tf_op jit(solution)/shard_map/feature_partials/pallas_call | solution.py:159
  30.0 24.5 %all_to_all.14 = f32[256,1,128]{2,1,0:T(1,128)S(1)} all-to-all(f32[256,1,128]{2,1,0:T(1,128)} %bitcast.10), channel_id=1, replica_groups=mesh['row'=16,'col'=16] {'row','col'}, dimensions={0} | all-to-all | bytes 262144 | tf_op jit(solution)/shard_map/all_to_all | solution.py:167
  54.5 0.1 reduce_sum.9
  54.5 0.7 %reshape.10 = f32[4,2,64]{2,1,0:T(2,128)} reshape(f32[4,128]{1,0:T(4,128)S(1)} %reduce_sum.9) | data formatting | bytes 4096 | tf_op jit(solution)/shard_map/reshape | solution.py:169
Async XLA Ops:
  3.0 24.2 %all-to-all-start = ((f32[16,32,128]{2,1,0:T(8,128)}), f32[16,32,128]{2,1,0:T(8,128)S(1)}, u32[]{:S(2)}, u32[]{:S(2)}) async-start(f32[16,32,128]{2,1,0:T(8,128)} %input_terms.1), calls=%async_computation | async-start | bytes 524288 | tf_op jit(solution)/shard_map/all_to_all | solution.py:158
  19.0 4.0 %collective-permute-start = (f32[64,128]{1,0:T(8,128)}, f32[64,128]{1,0:T(8,128)S(1)}, u32[]{:S(2)}, u32[]{:S(2)}) collective-permute-start(f32[64,128]{1,0:T(8,128)} %get-tuple-element.10), channel_id=1, source_target_pairs={{0,1},{1,0},{2,3},{3,2},{4,5},{5,4},{6,7},{7,6},{8,9},{9,8},{10,11... | collective-permute-start | bytes 98312 | tf_op jit(solution)/shard_map/ppermute | solution.py:155
  20.3 5.1 %collective-permute-start.1 = (f32[64,128]{1,0:T(8,128)}, f32[64,128]{1,0:T(8,128)S(1)}, u32[]{:S(2)}, u32[]{:S(2)}) collective-permute-start(f32[64,128]{1,0:T(8,128)} %get-tuple-element.11), channel_id=1, source_target_pairs={{0,2},{1,3},{2,0},{3,1},{4,6},{5,7},{6,4},{7,5},{8,10},{9,11},{10,... | collective-permute-start | bytes 98312 | tf_op jit(solution)/shard_map/ppermute | solution.py:155
  22.7 4.5 %collective-permute-start.2 = (f32[64,128]{1,0:T(8,128)}, f32[64,128]{1,0:T(8,128)S(1)}, u32[]{:S(2)}, u32[]{:S(2)}) collective-permute-start(f32[64,128]{1,0:T(8,128)} %get-tuple-element.12), channel_id=1, source_target_pairs={{0,3},{1,2},{2,1},{3,0},{4,7},{5,6},{6,5},{7,4},{8,11},{9,10},{10,... | collective-permute-start | bytes 98312 | tf_op jit(solution)/shard_map/ppermute | solution.py:155
  22.9 4.3 %copy-start.1 = (f32[64,128]{1,0:T(8,128)}, f32[64,128]{1,0:T(8,128)S(1)}, u32[]{:S(2)}) copy-start(f32[64,128]{1,0:T(8,128)S(1)} %collective-permute-done.near) | copy-start | bytes 98308
  25.4 1.9 %copy-start.2 = (f32[64,128]{1,0:T(8,128)}, f32[64,128]{1,0:T(8,128)S(1)}, u32[]{:S(2)}) copy-start(f32[64,128]{1,0:T(8,128)S(1)} %collective-permute-done.1.far) | copy-start | bytes 98308
  27.2 0.6 %copy-start.3 = (f32[64,128]{1,0:T(8,128)}, f32[64,128]{1,0:T(8,128)S(1)}, u32[]{:S(2)}) copy-start(f32[64,128]{1,0:T(8,128)S(1)} %collective-permute-done.2.both) | copy-start | bytes 98308
  27.2 0.7 %copy-start = (f32[16,32,128]{2,1,0:T(8,128)}, f32[16,32,128]{2,1,0:T(8,128)S(1)}, u32[]{:S(2)}) copy-start(f32[16,32,128]{2,1,0:T(8,128)S(1)} %all-to-all-done.terms) | copy-start | bytes 786436

commit v2 on v1

v2 whole, which is shorter than its diff:
```python
import jax
import jax.numpy as jnp
from jax import lax
from jax.experimental import pallas as pl
from jax.experimental.pallas import tpu as pltpu
from jax.sharding import Mesh, PartitionSpec as P

D = 5120
FF = 13824
K_IN = 32
K_OUT = 64
SEQ_LEN = 2048
SEQS = 4
LANES = 128
BLOCKS = SEQ_LEN // LANES
IN_HERE = 8
OUT_HERE = 32
MULTIPLIER = 73244475
AXES = ("zh", "y", "core", "zl", "x")
SIZES = (2, 4, 2, 4, 4)
ROW = ("zh", "y", "core")
COL = ("zl", "x")

SIN_TURN = (
    6.283185280154403,
    -41.34168061334532,
    81.60247636883796,
    -76.5811726421402,
    39.75982706857711,
)


def scramble(counter, seed_value):
    hashed = counter ^ seed_value
    hashed = hashed * jnp.int32(MULTIPLIER)
    hashed = hashed ^ lax.shift_right_logical(hashed, jnp.full_like(hashed, 16))
    hashed = hashed * jnp.int32(MULTIPLIER)
    return hashed ^ lax.shift_right_logical(hashed, jnp.full_like(hashed, 16))


def unit_draw(hashed):
    top_bits = lax.shift_right_logical(hashed, jnp.full_like(hashed, 8))
    return (top_bits.astype(jnp.float32) + 0.5) * (1.0 / 16777216.0)


def cos_turn(angle):
    quarter = jnp.abs(angle - 0.5) - 0.25
    square = quarter * quarter
    total = jnp.full_like(square, SIN_TURN[-1])
    for term in SIN_TURN[-2::-1]:
        total = total * square + term
    return total * quarter


def normal_draw(counter, seed_value, fan_in):
    radius = jnp.sqrt(-2.0 * jnp.log(unit_draw(scramble(2 * counter, seed_value))))
    angle = unit_draw(scramble(2 * counter + 1, seed_value))
    return (radius * cos_turn(angle) * fan_in ** (-0.5)).astype(jnp.bfloat16)


def input_kernel(seeds, offsets, acts, send, keep, held, blocks, arrived):
    zh, y, core, zl, x = (lax.axis_index(axis) for axis in AXES)
    here = acts.shape[1]
    fetch = pltpu.make_async_copy(acts.at[x], held, arrived)
    fetch.start()
    shape = (IN_HERE, here)
    factor = zl * IN_HERE + lax.broadcasted_iota(jnp.int32, shape, 0)
    row = (zh * 4 + y) * 2 + core
    feature = row * here + lax.broadcasted_iota(jnp.int32, shape, 1)
    table = normal_draw(offsets[0] + feature * K_IN + factor, seeds[0], D)
    fetch.wait()
    for part in range(4):
        product = jnp.dot(
            table, held[:, part * 512 : (part + 1) * 512], preferred_element_type=jnp.float32
        )
        for piece in range(4):
            blocks[part * 4 + piece] = product[:, piece * LANES : (piece + 1) * LANES]
    for out, other in ((send, core ^ 1), (keep, core)):
        for b in range(2):
            for c in range(2):
                for z in range(2):
                    out[b, c, z] = blocks[(z * 4 + (y ^ b ^ (3 * c))) * 2 + other]


def output_kernel(seeds, offsets, grads, send, keep):
    zl, x = (lax.axis_index(axis) for axis in COL)
    here = grads.shape[1]
    shape = (K_OUT, here)
    factor = lax.broadcasted_iota(jnp.int32, shape, 0)
    feature = (zl * 4 + x) * here + lax.broadcasted_iota(jnp.int32, shape, 1)
    table = normal_draw(offsets[1] + feature * K_OUT + factor, seeds[1], FF)
    for b, out in ((1, send), (0, keep)):
        for c in range(2):
            out[c] = jnp.dot(
                table, grads[x ^ b ^ (3 * c)], preferred_element_type=jnp.float32
            )


def pack_kernel(in_own, in_other, out_own, out_other, packed):
    side_in = in_own[0] + in_other[...]
    side_out = out_own[0] + out_other[...]
    for dest in range(8):
        half = (dest // 4) * OUT_HERE
        packed[dest, :OUT_HERE] = side_out[half : half + OUT_HERE]
        for z in range(2):
            start = OUT_HERE + z * IN_HERE
            packed[dest, start : start + IN_HERE] = side_in[z]


def feature_kernel(packed, spread):
    zl = lax.axis_index("zl")
    total = None
    for z in range(2):
        source = z * 4
        side_out = (packed[source, :OUT_HERE] + packed[source + 1, :OUT_HERE]) + (
            packed[source + 2, :OUT_HERE] + packed[source + 3, :OUT_HERE]
        )
        start = OUT_HERE + z * IN_HERE
        rows = pl.ds(start, IN_HERE)
        side_in = packed[zl, rows, :] + packed[4 + zl, rows, :]
        product = lax.dot_general(
            side_in,
            jnp.concatenate([side_out] * 4, axis=0),
            (((1,), (1,)), ((), ())),
            precision=lax.Precision.HIGHEST,
            preferred_element_type=jnp.float32,
        )
        total = product if total is None else total + product
    total = total * SEQ_LEN ** (-0.5)
    for place in range(8):
        spread[place] = total if place == 0 else pltpu.roll(total, LANES - 4 * place, 1)


def body(activations, out_grads, hash_seeds, offsets):
    acts = jnp.swapaxes(activations, 1, 2)
    grads = jnp.swapaxes(out_grads, 1, 2)
    here_in = acts.shape[1]
    smem = pl.BlockSpec(memory_space=pltpu.SMEM)
    vmem = pl.BlockSpec(memory_space=pltpu.VMEM)
    small = pltpu.CompilerParams(vmem_limit_bytes=16 * 1024 * 1024)

    def shaped(*dims):
        return jax.ShapeDtypeStruct(dims, jnp.float32)

    def swap(value, axis, distance):
        size = SIZES[AXES.index(axis)]
        return lax.ppermute(value, axis, [(i, i ^ distance) for i in range(size)])

    in_send, in_keep = pl.pallas_call(
        input_kernel,
        out_shape=[shaped(2, 2, 2, IN_HERE, LANES)] * 2,
        in_specs=[smem, smem, pl.BlockSpec(memory_space=pl.ANY)],
        out_specs=[vmem] * 2,
        scratch_shapes=[
            pltpu.VMEM((here_in, SEQ_LEN), jnp.bfloat16),
            pltpu.VMEM((BLOCKS, IN_HERE, LANES), jnp.float32),
            pltpu.SemaphoreType.DMA,
        ],
        compiler_params=pltpu.CompilerParams(vmem_limit_bytes=60 * 1024 * 1024),
        name="input_terms",
    )(hash_seeds, offsets, acts)
    in_got = swap(in_send, "core", 1)
    out_send, out_keep = pl.pallas_call(
        output_kernel,
        out_shape=[shaped(2, K_OUT, LANES)] * 2,
        in_specs=[smem, smem, vmem],
        out_specs=[vmem] * 2,
        compiler_params=small,
        name="output_terms",
    )(hash_seeds, offsets, grads)
    in_sum = in_keep + in_got
    in_pair = in_sum[0] + swap(in_sum[1], "y", 1)
    out_pair = out_keep + swap(out_send, "x", 1)
    in_got = swap(in_pair[1], "y", 3)
    out_got = swap(out_pair[1], "x", 3)
    packed = pl.pallas_call(
        pack_kernel,
        out_shape=shaped(8, OUT_HERE + 2 * IN_HERE, LANES),
        in_specs=[vmem] * 4,
        out_specs=vmem,
        compiler_params=small,
        name="pack_sides",
    )(in_pair, in_got, out_pair, out_got)
    packed = lax.all_to_all(packed, ("zh", "zl"), 0, 0, tiled=True)
    spread = pl.pallas_call(
        feature_kernel,
        out_shape=shaped(8, 8, LANES),
        in_specs=[vmem],
        out_specs=vmem,
        compiler_params=small,
        name="feature_partials",
    )(packed)
    spread = lax.all_to_all(
        spread.reshape(32, 2, LANES), ("y", "core", "x"), 0, 0, tiled=True
    )
    summed = jnp.sum(spread.reshape(8, SEQS, 2, LANES), axis=0)
    return summed[:, :, :4]


def solution(mesh):
    fine = Mesh(mesh.devices.reshape(SIZES), AXES)
    return jax.shard_map(
        body,
        mesh=fine,
        in_specs=(P(None, None, ROW), P(None, ROW, COL), P(), P()),
        out_specs=P(None, COL, ROW),
        check_vma=False,
    )
```

time: 55.5 us -> 52.1 us (0.939)
  starting transfers between devices: 16.6 us -> 8.16 us
  blocking collectives: 24.5 us -> 32 us
  Pallas kernels: 8.38 us -> 4.64 us
  local copies, waits for them, and re-layouts: 1.38 us -> 0.02 us
  other arithmetic: 0.08 us -> 1.39 us
  waiting for transfers between devices: 4.28 us -> 5.54 us
    all_to_all x1 -> x0, starting transfers between devices: 12.6 us -> none  [body(): terms = lax.all_to_all(terms, 'row', 0, 0, tiled=True)]
    all_to_all x1 -> x2, blocking collectives: 24.5 us -> 32 us  [the longest x1 16.7 us: body(): packed = lax.all_to_all(packed, ('zh', 'zl'), 0, 0, tiled=True)]
    ppermute x3 -> x5, starting transfers between devices: 3.97 us -> 8.16 us  [swap(): return lax.ppermute(value, axis, [(i, i ^ distance) for i in range(size)])]
    pallas_call x3 -> x4, Pallas kernels: 8.38 us -> 4.64 us  [the longest x1 3.08 us: body(): pl.pallas_call(input_kernel, out_shape=[shaped(2, 2, 2, IN_HERE, LANES)]...]
    ppermute x3 -> x5, waiting for transfers between devices: 4.28 us -> 5.54 us  [swap(): return lax.ppermute(value, axis, [(i, i ^ distance) for i in range(size)])]
    add x0 -> x3, other arithmetic: none -> 0.78 us  [the longest x1 0.76 us: body(): in_sum = in_keep + in_got]
    unnamed x8 -> x6, local copies, waits for them, and re-layouts: 0.7 us -> 0.01 us
    reshape x1 -> x0, local copies, waits for them, and re-layouts: 0.68 us -> none  [body(): return summed.reshape(SEQS, 2, K_OUT)[:, :, :4]]
  transfers between devices with their start and end apart: 4 -> 5, of which waited for: 2 -> 4; matrix products, arithmetic and copies ran while one was open for 0% -> 0% of each run, Pallas kernels for 6% -> 2%
where the time goes in v2:
time: 52.1 us; the launch traced here: 51.8 us
  blocking collectives  32 us (61%)
  starting transfers between devices  8.16 us (16%)
  waiting for transfers between devices  5.54 us (11%)
  Pallas kernels  4.64 us (9%)
  other arithmetic  1.39 us (3%)
    all_to_all x1, blocking collectives, body(): packed = lax.all_to_all(packed, ('zh', 'zl'), 0, 0, tiled=True)  16.7 us
    all_to_all x1, blocking collectives, body(): lax.all_to_all(spread.reshape(32, 2, LANES), ('y', 'core', 'x'), 0, 0, ti...  15.3 us
    ppermute x5, starting transfers between devices, swap(): return lax.ppermute(value, axis, [(i, i ^ distance) for i in range(size)])  8.16 us
    ppermute x5, waiting for transfers between devices, swap(): return lax.ppermute(value, axis, [(i, i ^ distance) for i in range(size)])  5.54 us
    pallas_call x1, Pallas kernels, body(): pl.pallas_call(input_kernel, out_shape=[shaped(2, 2, 2, IN_HERE, LANES)]...  3.08 us
    pallas_call x1, Pallas kernels, body(): pl.pallas_call(output_kernel, out_shape=[shaped(2, K_OUT, LANES)] * 2, in...  1.17 us
  transfers between devices with their start and end apart: 5, of which 4 were waited for; matrix products, arithmetic and copies ran while one was open for 0% of the time, Pallas kernels for 2%

profile of v2, /device:TPU:1, one launch (start us, length us, event | category | flops | bytes accessed | tf_op | source)
XLA Modules:
  0.0 51.8 jit_solution(15978037760641678118)
XLA Ops:
  0.0 0.0 copy-start.2
  0.0 0.0 copy-start.1
  0.0 0.0 copy-start
  0.0 3.1 %input_terms.1 = (f32[2,2,2,8,128]{4,3,2,1,0:T(8,128)}, f32[2,2,2,8,128]{4,3,2,1,0:T(8,128)}) custom-call(s32[2]{0:T(128)} %seeds.3, s32[2]{0:T(128)} %offsets.3, bf16[4,320,2048]{2,1,0:T(8,128)(2,1)} %bitcast.17), custom_call_target="tpu_custom_call" | custom-call | tf_op jit(solution)/shard_map/input_terms/pallas_call | solution.py:149
  3.1 3.3 %collective-permute-start = (f32[2,2,2,8,128]{4,3,2,1,0:T(8,128)}, f32[2,2,2,8,128]{4,3,2,1,0:T(8,128)S(1)}, u32[]{:S(2)}, u32[]{:S(2)}) collective-permute-start(f32[2,2,2,8,128]{4,3,2,1,0:T(8,128)} %get-tuple-element.10), channel_id=1, source_target_pairs={{0,16},{16,0},{1,17},{17,1},{2,18},{18,2},{3,19},{19,3},{4,20},{20... | collective-permute-start | bytes 98312 | tf_op jit(solution)/shard_map/ppermute | solution.py:147
  6.4 1.1 %collective-permute-done = f32[2,2,2,8,128]{4,3,2,1,0:T(8,128)S(1)} collective-permute-done((f32[2,2,2,8,128]{4,3,2,1,0:T(8,128)}, f32[2,2,2,8,128]{4,3,2,1,0:T(8,128)S(1)}, u32[]{:S(2)}, u32[]{:S(2)}) %collective-permute-start) | collective-permute-done | bytes 32800 | tf_op jit(solution)/shard_map/ppermute | solution.py:147
  7.5 0.8 %add.9 = f32[2,2,2,8,128]{4,3,2,1,0:T(8,128)S(1)} add(f32[2,2,2,8,128]{4,3,2,1,0:T(8,128)} %get-tuple-element.9, f32[2,2,2,8,128]{4,3,2,1,0:T(8,128)S(1)} %collective-permute-done) | non-fusion elementwise | flops 8192 | bytes 98304 | tf_op jit(solution)/shard_map/add | solution.py:171
  8.3 0.0 collective-permute-start.1
  8.3 0.0 copy-done.2
  8.3 0.0 copy-done.1
  8.3 0.0 copy-done
  8.3 1.2 %output_terms.1 = (f32[2,64,128]{2,1,0:T(8,128)S(1)}, f32[2,64,128]{2,1,0:T(8,128)S(1)}) custom-call(s32[2]{0:T(128)S(1)} %copy-done.1, s32[2]{0:T(128)S(1)} %copy-done.2, bf16[4,864,128]{2,1,0:T(8,128)(2,1)S(1)} %bitcast.15), custom_call_target="tpu_custom_call" | custom-call | tf_op jit(solution)/shard_map/output_terms/pallas_call | solution.py:163
  9.5 0.8 %collective-permute-start.3 = (f32[2,64,128]{2,1,0:T(8,128)S(1)}, f32[2,64,128]{2,1,0:T(8,128)S(1)}, u32[]{:S(2)}, u32[]{:S(2)}) collective-permute-start(f32[2,64,128]{2,1,0:T(8,128)S(1)} %get-tuple-element.12), channel_id=1, source_target_pairs={{0,1},{1,0},{2,3},{3,2},{4,5},{5,4},{6,7},{7,6},{8,9},{9,8},{10,11... | collective-permute-start | bytes 196616 | tf_op jit(solution)/shard_map/ppermute | solution.py:147
  10.3 0.5 %collective-permute-done.1 = f32[2,2,8,128]{3,2,1,0:T(8,128)S(1)} collective-permute-done((f32[2,2,8,128]{3,2,1,0:T(8,128)S(1)}, f32[2,2,8,128]{3,2,1,0:T(8,128)S(1)}, u32[]{:S(2)}, u32[]{:S(2)}) %collective-permute-start.1) | collective-permute-done | bytes 16416 | tf_op jit(solution)/shard_map/ppermute | solution.py:147
  10.9 1.8 %collective-permute-done.3 = f32[2,64,128]{2,1,0:T(8,128)S(1)} collective-permute-done((f32[2,64,128]{2,1,0:T(8,128)S(1)}, f32[2,64,128]{2,1,0:T(8,128)S(1)}, u32[]{:S(2)}, u32[]{:S(2)}) %collective-permute-start.3) | collective-permute-done | bytes 65568 | tf_op jit(solution)/shard_map/ppermute | solution.py:147
  12.7 2.1 %collective-permute-start.4 = (f32[64,128]{1,0:T(8,128)S(1)}, f32[64,128]{1,0:T(8,128)S(1)}, u32[]{:S(2)}, u32[]{:S(2)}) collective-permute-start(f32[64,128]{1,0:T(8,128)S(1)} %slice_bitcast_fusion), channel_id=1, source_target_pairs={{0,3},{1,2},{2,1},{3,0},{4,7},{5,6},{6,5},{7,4},{8,11},{9,10},{10,... | collective-permute-start | bytes 98312 | tf_op jit(solution)/shard_map/ppermute | solution.py:147
  14.8 1.9 %collective-permute-start.2 = (f32[2,8,128]{2,1,0:T(8,128)S(1)}, f32[2,8,128]{2,1,0:T(8,128)S(1)}, u32[]{:S(2)}, u32[]{:S(2)}) collective-permute-start(f32[2,8,128]{2,1,0:T(8,128)S(1)} %slice_bitcast_fusion.3), channel_id=1, source_target_pairs={{0,96},{32,64},{64,32},{96,0},{1,97},{33,65},{65,33},{97,1},{2,98}... | collective-permute-start | bytes 24584 | tf_op jit(solution)/shard_map/ppermute | solution.py:147
  16.7 2.1 %collective-permute-done.2.in_other = f32[2,8,128]{2,1,0:T(8,128)S(1)} collective-permute-done((f32[2,8,128]{2,1,0:T(8,128)S(1)}, f32[2,8,128]{2,1,0:T(8,128)S(1)}, u32[]{:S(2)}, u32[]{:S(2)}) %collective-permute-start.2) | collective-permute-done | bytes 8224 | tf_op jit(solution)/shard_map/ppermute | solution.py:147
  18.8 0.0 collective-permute-done.4.out_other
  18.8 16.7 %all_to_all.10.packed = f32[8,48,128]{2,1,0:T(8,128)S(1)} all-to-all(f32[8,48,128]{2,1,0:T(8,128)S(1)} %pack_sides.1), channel_id=1, replica_groups=mesh['zh'=2,'y'=4,'core'=2,'zl'=4,'x'=4] {'zh','zl'}, dimensions={0} | all-to-all | bytes 393216 | tf_op jit(solution)/shard_map/all_to_all | solution.py:184
  35.6 0.4 feature_partials.1
  35.9 15.3 %all_to_all.11 = f32[32,2,128]{2,1,0:T(2,128)S(1)} all-to-all(f32[32,2,128]{2,1,0:T(2,128)S(1)} %bitcast.16), channel_id=1, replica_groups=mesh['zh'=2,'y'=4,'core'=2,'zl'=4,'x'=4] {'y','core','x'}, dimensions={0} | all-to-all | bytes 65536 | tf_op jit(solution)/shard_map/all_to_all | solution.py:193
  51.2 0.6 %reduce_sum.9 = f32[4,2,128]{2,1,0:T(2,128)} reduce(f32[8,4,2,128]{3,2,1,0:T(2,128)S(1)} %bitcast.18, f32[]{:T(128)} %constant.0.clone.1), dimensions={0}, to_apply=%region_0.0 | reduce | flops 7168 | bytes 36868 | tf_op jit(solution)/shard_map/reduce_sum | solution.py:196
  (6 shorter events, 0.0 us)
Async XLA Ops:
  0.0 8.3 %copy-start.2 = (s32[2]{0:T(128)S(1)}, s32[2]{0:T(128)}, u32[]{:S(2)}) copy-start(s32[2]{0:T(128)} %offsets.3) | copy-start | bytes 28
  0.0 8.3 %copy-start.1 = (s32[2]{0:T(128)S(1)}, s32[2]{0:T(128)}, u32[]{:S(2)}) copy-start(s32[2]{0:T(128)} %seeds.3) | copy-start | bytes 28
  0.0 8.3 %copy-start = (bf16[4,128,864]{1,2,0:T(8,128)(2,1)S(1)}, bf16[4,128,864]{1,2,0:T(8,128)(2,1)}, u32[]{:S(2)}) copy-start(bf16[4,128,864]{1,2,0:T(8,128)(2,1)} %param.5) | copy-start | bytes 2654212
  3.1 4.4 %collective-permute-start = (f32[2,2,2,8,128]{4,3,2,1,0:T(8,128)}, f32[2,2,2,8,128]{4,3,2,1,0:T(8,128)S(1)}, u32[]{:S(2)}, u32[]{:S(2)}) collective-permute-start(f32[2,2,2,8,128]{4,3,2,1,0:T(8,128)} %get-tuple-element.10), channel_id=1, source_target_pairs={{0,16},{16,0},{1,17},{17,1},{2,18},{18,2},{3,19},{19,3},{4,20},{20... | collective-permute-start | bytes 98312 | tf_op jit(solution)/shard_map/ppermute | solution.py:147
  8.3 2.6 %collective-permute-start.1 = (f32[2,2,8,128]{3,2,1,0:T(8,128)S(1)}, f32[2,2,8,128]{3,2,1,0:T(8,128)S(1)}, u32[]{:S(2)}, u32[]{:S(2)}) collective-permute-start(f32[2,2,8,128]{3,2,1,0:T(8,128)S(1)} %slice_bitcast_fusion.1), channel_id=1, source_target_pairs={{0,32},{32,0},{64,96},{96,64},{1,33},{33,1},{65,97},{97,65},{2,34}... | collective-permute-start | bytes 49160 | tf_op jit(solution)/shard_map/ppermute | solution.py:147
  9.5 3.2 %collective-permute-start.3 = (f32[2,64,128]{2,1,0:T(8,128)S(1)}, f32[2,64,128]{2,1,0:T(8,128)S(1)}, u32[]{:S(2)}, u32[]{:S(2)}) collective-permute-start(f32[2,64,128]{2,1,0:T(8,128)S(1)} %get-tuple-element.12), channel_id=1, source_target_pairs={{0,1},{1,0},{2,3},{3,2},{4,5},{5,4},{6,7},{7,6},{8,9},{9,8},{10,11... | collective-permute-start | bytes 196616 | tf_op jit(solution)/shard_map/ppermute | solution.py:147
  12.7 6.1 %collective-permute-start.4 = (f32[64,128]{1,0:T(8,128)S(1)}, f32[64,128]{1,0:T(8,128)S(1)}, u32[]{:S(2)}, u32[]{:S(2)}) collective-permute-start(f32[64,128]{1,0:T(8,128)S(1)} %slice_bitcast_fusion), channel_id=1, source_target_pairs={{0,3},{1,2},{2,1},{3,0},{4,7},{5,6},{6,5},{7,4},{8,11},{9,10},{10,... | collective-permute-start | bytes 98312 | tf_op jit(solution)/shard_map/ppermute | solution.py:147
  14.8 4.0 %collective-permute-start.2 = (f32[2,8,128]{2,1,0:T(8,128)S(1)}, f32[2,8,128]{2,1,0:T(8,128)S(1)}, u32[]{:S(2)}, u32[]{:S(2)}) collective-permute-start(f32[2,8,128]{2,1,0:T(8,128)S(1)} %slice_bitcast_fusion.3), channel_id=1, source_target_pairs={{0,96},{32,64},{64,32},{96,0},{1,97},{33,65},{65,33},{97,1},{2,98}... | collective-permute-start | bytes 24584 | tf_op jit(solution)/shard_map/ppermute | solution.py:147

commit v3 on v2

--- a/solution.py
+++ b/solution.py
@@ -14,6 +14,9 @@
 LANES = 128
 BLOCKS = SEQ_LEN // LANES
 IN_HERE = 8
+IN_SENT = 16
+PARTS = 2
+PART = SEQ_LEN // 2 // PARTS
 OUT_HERE = 32
 MULTIPLIER = 73244475
 AXES = ("zh", "y", "core", "zl", "x")
@@ -58,31 +61,47 @@
     return (radius * cos_turn(angle) * fan_in ** (-0.5)).astype(jnp.bfloat16)
 
 
-def input_kernel(seeds, offsets, acts, send, keep, held, blocks, arrived):
+def input_kernel(
+    seeds_hbm, offsets_hbm, acts, send, keep, seeds, offsets, held, blocks, arrived, told
+):
     zh, y, core, zl, x = (lax.axis_index(axis) for axis in AXES)
     here = acts.shape[1]
-    fetch = pltpu.make_async_copy(acts.at[x], held, arrived)
-    fetch.start()
-    shape = (IN_HERE, here)
-    factor = zl * IN_HERE + lax.broadcasted_iota(jnp.int32, shape, 0)
+    half = lax.shift_right_logical(zl, 1)
+    tell = [
+        pltpu.make_async_copy(seeds_hbm, seeds, told.at[0]),
+        pltpu.make_async_copy(offsets_hbm, offsets, told.at[1]),
+    ]
+    for copy in tell:
+        copy.start()
+    fetches = []
+    for part in range(PARTS):
+        start = pl.multiple_of(half * (SEQ_LEN // 2) + part * PART, PART)
+        fetch = pltpu.make_async_copy(
+            acts.at[x, :, pl.ds(start, PART)], held.at[part], arrived.at[part]
+        )
+        fetch.start()
+        fetches.append(fetch)
+    for copy in tell:
+        copy.wait()
+    shape = (IN_SENT, here)
+    factor = (zl & 1) * IN_SENT + lax.broadcasted_iota(jnp.int32, shape, 0)
     row = (zh * 4 + y) * 2 + core
     feature = row * here + lax.broadcasted_iota(jnp.int32, shape, 1)
     table = normal_draw(offsets[0] + feature * K_IN + factor, seeds[0], D)
-    fetch.wait()
-    for part in range(4):
-        product = jnp.dot(
-            table, held[:, part * 512 : (part + 1) * 512], preferred_element_type=jnp.float32
-        )
-        for piece in range(4):
-            blocks[part * 4 + piece] = product[:, piece * LANES : (piece + 1) * LANES]
+    for part in range(PARTS):
+        fetches[part].wait()
+        product = jnp.dot(table, held[part], preferred_element_type=jnp.float32)
+        for piece in range(PART // LANES):
+            blocks[part * (PART // LANES) + piece] = product[
+                :, piece * LANES : (piece + 1) * LANES
+            ]
     for out, other in ((send, core ^ 1), (keep, core)):
         for b in range(2):
             for c in range(2):
-                for z in range(2):
-                    out[b, c, z] = blocks[(z * 4 + (y ^ b ^ (3 * c))) * 2 + other]
-
-
-def output_kernel(seeds, offsets, grads, send, keep):
+                out[b, c] = blocks[(y ^ b ^ (3 * c)) * 2 + other]
+
+
+def output_kernel(seeds, offsets, grads, after, send, keep):
     zl, x = (lax.axis_index(axis) for axis in COL)
     here = grads.shape[1]
     shape = (K_OUT, here)
@@ -96,28 +115,31 @@
             )
 
 
-def pack_kernel(in_own, in_other, out_own, out_other, packed):
-    side_in = in_own[0] + in_other[...]
-    side_out = out_own[0] + out_other[...]
+def add_kernel(own, got, after, send, keep):
+    keep[...] = own[0] + got[0]
+    send[...] = own[1] + got[1]
+
+
+def pack_kernel(in_own, in_got, out_own, out_got, packed):
+    side_in = in_own[...] + in_got[...]
+    side_out = out_own[...] + out_got[...]
     for dest in range(8):
         half = (dest // 4) * OUT_HERE
         packed[dest, :OUT_HERE] = side_out[half : half + OUT_HERE]
-        for z in range(2):
-            start = OUT_HERE + z * IN_HERE
-            packed[dest, start : start + IN_HERE] = side_in[z]
+        half = (dest % 2) * IN_HERE
+        packed[dest, OUT_HERE:] = side_in[half : half + IN_HERE]
 
 
 def feature_kernel(packed, spread):
-    zl = lax.axis_index("zl")
+    factor_half = lax.shift_right_logical(lax.axis_index("zl"), 1)
     total = None
     for z in range(2):
         source = z * 4
         side_out = (packed[source, :OUT_HERE] + packed[source + 1, :OUT_HERE]) + (
             packed[source + 2, :OUT_HERE] + packed[source + 3, :OUT_HERE]
         )
-        start = OUT_HERE + z * IN_HERE
-        rows = pl.ds(start, IN_HERE)
-        side_in = packed[zl, rows, :] + packed[4 + zl, rows, :]
+        source = z * 2 + factor_half
+        side_in = packed[source, OUT_HERE:] + packed[4 + source, OUT_HERE:]
         product = lax.dot_general(
             side_in,
             jnp.concatenate([side_out] * 4, axis=0),
@@ -137,57 +159,77 @@
     here_in = acts.shape[1]
     smem = pl.BlockSpec(memory_space=pltpu.SMEM)
     vmem = pl.BlockSpec(memory_space=pltpu.VMEM)
-    small = pltpu.CompilerParams(vmem_limit_bytes=16 * 1024 * 1024)
+    hbm = pl.BlockSpec(memory_space=pltpu.HBM)
+    anywhere = pl.BlockSpec(memory_space=pl.ANY)
+    params = pltpu.CompilerParams(vmem_limit_bytes=16 * 1024 * 1024)
 
     def shaped(*dims):
         return jax.ShapeDtypeStruct(dims, jnp.float32)
+
+    def pinned(value):
+        return pltpu.with_memory_space_constraint(value, pltpu.HBM)
 
     def swap(value, axis, distance):
         size = SIZES[AXES.index(axis)]
         return lax.ppermute(value, axis, [(i, i ^ distance) for i in range(size)])
 
+    def add(own, got, after, name):
+        return pl.pallas_call(
+            add_kernel,
+            out_shape=[shaped(*own.shape[1:])] * 2,
+            in_specs=[vmem, vmem, anywhere],
+            out_specs=[vmem] * 2,
+            compiler_params=params,
+            name=name,
+        )(own, got, after)
+
     in_send, in_keep = pl.pallas_call(
         input_kernel,
-        out_shape=[shaped(2, 2, 2, IN_HERE, LANES)] * 2,
-        in_specs=[smem, smem, pl.BlockSpec(memory_space=pl.ANY)],
+        out_shape=[shaped(2, 2, IN_SENT, LANES)] * 2,
+        in_specs=[hbm] * 3,
         out_specs=[vmem] * 2,
         scratch_shapes=[
-            pltpu.VMEM((here_in, SEQ_LEN), jnp.bfloat16),
-            pltpu.VMEM((BLOCKS, IN_HERE, LANES), jnp.float32),
-            pltpu.SemaphoreType.DMA,
+            pltpu.SMEM((2,), jnp.int32),
+            pltpu.SMEM((2,), jnp.int32),
+            pltpu.VMEM((PARTS, here_in, PART), jnp.bfloat16),
+            pltpu.VMEM((BLOCKS // 2, IN_SENT, LANES), jnp.float32),
+            pltpu.SemaphoreType.DMA((PARTS,)),
+            pltpu.SemaphoreType.DMA((2,)),
         ],
-        compiler_params=pltpu.CompilerParams(vmem_limit_bytes=60 * 1024 * 1024),
+        compiler_params=params,
         name="input_terms",
-    )(hash_seeds, offsets, acts)
+    )(pinned(hash_seeds), pinned(offsets), pinned(acts))
     in_got = swap(in_send, "core", 1)
     out_send, out_keep = pl.pallas_call(
         output_kernel,
         out_shape=[shaped(2, K_OUT, LANES)] * 2,
-        in_specs=[smem, smem, vmem],
+        in_specs=[smem, smem, vmem, anywhere],
         out_specs=[vmem] * 2,
-        compiler_params=small,
+        compiler_params=params,
         name="output_terms",
-    )(hash_seeds, offsets, grads)
-    in_sum = in_keep + in_got
-    in_pair = in_sum[0] + swap(in_sum[1], "y", 1)
-    out_pair = out_keep + swap(out_send, "x", 1)
-    in_got = swap(in_pair[1], "y", 3)
-    out_got = swap(out_pair[1], "x", 3)
+    )(hash_seeds, offsets, grads, in_send)
+    in_send, in_keep = add(in_keep, in_got, out_send, "add_core")
+    in_got = swap(in_send, "y", 1)
+    out_got = swap(out_send, "x", 1)
+    in_send, in_keep = add(in_keep, in_got, in_got, "add_y")
+    in_got = swap(in_send, "y", 3)
+    out_send, out_keep = add(out_keep, out_got, in_send, "add_x")
+    out_got = swap(out_send, "x", 3)
     packed = pl.pallas_call(
         pack_kernel,
-        out_shape=shaped(8, OUT_HERE + 2 * IN_HERE, LANES),
+        out_shape=shaped(8, OUT_HERE + IN_HERE, LANES),
         in_specs=[vmem] * 4,
         out_specs=vmem,
-        compiler_params=small,
+        compiler_params=params,
         name="pack_sides",
-    )(in_pair, in_got, out_pair, out_got)
+    )(in_keep, in_got, out_keep, out_got)
     packed = lax.all_to_all(packed, ("zh", "zl"), 0, 0, tiled=True)
     spread = pl.pallas_call(
         feature_kernel,
         out_shape=shaped(8, 8, LANES),
         in_specs=[vmem],
         out_specs=vmem,
-        compiler_params=small,
+        compiler_params=params,
         name="feature_partials",
     )(packed)
     spread = lax.all_to_all(

time: 52.1 us -> 48.7 us (0.935)
  waiting for transfers between devices: 5.54 us -> 3.81 us
  Pallas kernels: 4.64 us -> 3.02 us
  other arithmetic: 1.39 us -> 0.62 us
  blocking collectives: 32 us -> 32.6 us
    ppermute x5, waiting for transfers between devices: 5.54 us -> 3.81 us  [swap(): return lax.ppermute(value, axis, [(i, i ^ distance) for i in range(size)])]
    pallas_call x2 -> x5, Pallas kernels: 3.1 us -> 1.47 us  [the longest x1 1.43 us: body(): pl.pallas_call(input_kernel, out_shape=[shaped(2, 2, IN_SENT, LANES)] * 2...]
    add x3 -> x0, other arithmetic: 0.78 us -> none  [the longest x1 0.76 us: body(): in_sum = in_keep + in_got]
    all_to_all x1, blocking collectives: 15.3 us -> 16 us  [body(): lax.all_to_all(spread.reshape(32, 2, LANES), ('y', 'core', 'x'), 0, 0, ti...]
  transfers between devices with their start and end apart: 5 -> 5, of which waited for: 4 -> 3; matrix products, arithmetic and copies ran while one was open for 0% -> 0% of each run, Pallas kernels for 2% -> 0%
where the time goes in v3:
time: 48.7 us; the launch traced here: 48.5 us
  blocking collectives  32.6 us (67%)
  starting transfers between devices  8.4 us (17%)
  waiting for transfers between devices  3.81 us (8%)
  Pallas kernels  3.02 us (6%)
  other arithmetic  0.62 us (1%)
    all_to_all x1, blocking collectives, body(): packed = lax.all_to_all(packed, ('zh', 'zl'), 0, 0, tiled=True)  16.7 us
    all_to_all x1, blocking collectives, body(): lax.all_to_all(spread.reshape(32, 2, LANES), ('y', 'core', 'x'), 0, 0, ti...  16 us
    ppermute x5, starting transfers between devices, swap(): return lax.ppermute(value, axis, [(i, i ^ distance) for i in range(size)])  8.4 us
    ppermute x5, waiting for transfers between devices, swap(): return lax.ppermute(value, axis, [(i, i ^ distance) for i in range(size)])  3.81 us
    pallas_call x1, Pallas kernels, body(): pl.pallas_call(input_kernel, out_shape=[shaped(2, 2, IN_SENT, LANES)] * 2...  1.43 us
    pallas_call x1, Pallas kernels, body(): pl.pallas_call(output_kernel, out_shape=[shaped(2, K_OUT, LANES)] * 2, in...  1.17 us
  transfers between devices with their start and end apart: 5, of which 3 were waited for; matrix products, arithmetic and copies ran while one was open for 0% of the time, Pallas kernels for 0%

profile of v3, /device:TPU:1, one launch (start us, length us, event | category | flops | bytes accessed | tf_op | source)
XLA Modules:
  0.0 48.5 jit_solution(7141326752378611908)
XLA Ops:
  0.0 0.0 copy-start.2
  0.0 0.0 copy-start.1
  0.0 0.0 copy-start
  0.0 1.4 %input_terms.1 = (f32[2,2,16,128]{3,2,1,0:T(8,128)S(1)}, f32[2,2,16,128]{3,2,1,0:T(8,128)S(1)}) custom-call(s32[2]{0:T(128)} %seeds.1, s32[2]{0:T(128)} %offsets.1, bf16[4,320,2048]{2,1,0:T(8,128)(2,1)} %bitcast.7), custom_call_target="tpu_custom_call" | custom-call | tf_op jit(solution)/shard_map/input_terms/pallas_call | solution.py:186
  1.5 0.0 copy-done.2
  1.5 0.0 copy-done.1
  1.5 0.0 copy-done
  1.5 1.2 %output_terms.1 = (f32[2,64,128]{2,1,0:T(8,128)S(1)}, f32[2,64,128]{2,1,0:T(8,128)S(1)}) custom-call(s32[2]{0:T(128)S(1)} %copy-done.1, s32[2]{0:T(128)S(1)} %copy-done.2, bf16[4,864,128]{2,1,0:T(8,128)(2,1)S(1)} %bitcast.5, f32[2,2,16,128]{3,2,1,0:T(8,128)S(1)} %get-tuple-element.16.after), custom_call_target="tpu_custom_call" | custom-call | tf_op jit(solution)/shard_map/output_terms/pallas_call | solution.py:203
  2.7 2.1 %collective-permute-start.3 = (f32[2,64,128]{2,1,0:T(8,128)S(1)}, f32[2,64,128]{2,1,0:T(8,128)S(1)}, u32[]{:S(2)}, u32[]{:S(2)}) collective-permute-start(f32[2,64,128]{2,1,0:T(8,128)S(1)} %get-tuple-element.17.after), channel_id=1, source_target_pairs={{0,1},{1,0},{2,3},{3,2},{4,5},{5,4},{6,7},{7,6},{8,9},{9,8},{10,11... | collective-permute-start | bytes 196616 | tf_op jit(solution)/shard_map/ppermute | solution.py:174
  4.8 1.3 %collective-permute-start = (f32[2,2,16,128]{3,2,1,0:T(8,128)S(1)}, f32[2,2,16,128]{3,2,1,0:T(8,128)S(1)}, u32[]{:S(2)}, u32[]{:S(2)}) collective-permute-start(f32[2,2,16,128]{3,2,1,0:T(8,128)S(1)} %get-tuple-element.16.after), channel_id=1, source_target_pairs={{0,16},{16,0},{1,17},{17,1},{2,18},{18,2},{3,19},{19,3},{4,20},{20... | collective-permute-start | bytes 98312 | tf_op jit(solution)/shard_map/ppermute | solution.py:174
  6.1 0.9 %collective-permute-done.got = f32[2,2,16,128]{3,2,1,0:T(8,128)S(1)} collective-permute-done((f32[2,2,16,128]{3,2,1,0:T(8,128)S(1)}, f32[2,2,16,128]{3,2,1,0:T(8,128)S(1)}, u32[]{:S(2)}, u32[]{:S(2)}) %collective-permute-start) | collective-permute-done | bytes 32800 | tf_op jit(solution)/shard_map/ppermute | solution.py:174
  6.9 1.0 %collective-permute-start.1 = (f32[2,16,128]{2,1,0:T(8,128)S(1)}, f32[2,16,128]{2,1,0:T(8,128)S(1)}, u32[]{:S(2)}, u32[]{:S(2)}) collective-permute-start(f32[2,16,128]{2,1,0:T(8,128)S(1)} %get-tuple-element.19), channel_id=1, source_target_pairs={{0,32},{32,0},{64,96},{96,64},{1,33},{33,1},{65,97},{97,65},{2,34}... | collective-permute-start | bytes 49160 | tf_op jit(solution)/shard_map/ppermute | solution.py:174
  7.9 1.9 %collective-permute-done.1.got.after = f32[2,16,128]{2,1,0:T(8,128)S(1)} collective-permute-done((f32[2,16,128]{2,1,0:T(8,128)S(1)}, f32[2,16,128]{2,1,0:T(8,128)S(1)}, u32[]{:S(2)}, u32[]{:S(2)}) %collective-permute-start.1) | collective-permute-done | bytes 16416 | tf_op jit(solution)/shard_map/ppermute | solution.py:174
  9.8 0.0 collective-permute-done.3.got
  9.8 1.3 %collective-permute-start.4 = (f32[64,128]{1,0:T(8,128)S(1)}, f32[64,128]{1,0:T(8,128)S(1)}, u32[]{:S(2)}, u32[]{:S(2)}) collective-permute-start(f32[64,128]{1,0:T(8,128)S(1)} %get-tuple-element.24), channel_id=1, source_target_pairs={{0,3},{1,2},{2,1},{3,0},{4,7},{5,6},{6,5},{7,4},{8,11},{9,10},{10,... | collective-permute-start | bytes 98312 | tf_op jit(solution)/shard_map/ppermute | solution.py:174
  11.1 2.7 %collective-permute-start.2 = (f32[16,128]{1,0:T(8,128)S(1)}, f32[16,128]{1,0:T(8,128)S(1)}, u32[]{:S(2)}, u32[]{:S(2)}) collective-permute-start(f32[16,128]{1,0:T(8,128)S(1)} %get-tuple-element.21.after), channel_id=1, source_target_pairs={{0,96},{32,64},{64,32},{96,0},{1,97},{33,65},{65,33},{97,1},{2,98}... | collective-permute-start | bytes 24584 | tf_op jit(solution)/shard_map/ppermute | solution.py:174
  13.9 1.0 %collective-permute-done.2.in_got = f32[16,128]{1,0:T(8,128)S(1)} collective-permute-done((f32[16,128]{1,0:T(8,128)S(1)}, f32[16,128]{1,0:T(8,128)S(1)}, u32[]{:S(2)}, u32[]{:S(2)}) %collective-permute-start.2) | collective-permute-done | bytes 8224 | tf_op jit(solution)/shard_map/ppermute | solution.py:174
  14.9 0.0 collective-permute-done.4.out_got
  14.9 16.7 %all_to_all.10.packed = f32[8,40,128]{2,1,0:T(8,128)S(1)} all-to-all(f32[8,40,128]{2,1,0:T(8,128)S(1)} %pack_sides.1), channel_id=1, replica_groups=mesh['zh'=2,'y'=4,'core'=2,'zl'=4,'x'=4] {'zh','zl'}, dimensions={0} | all-to-all | bytes 327680 | tf_op jit(solution)/shard_map/all_to_all | solution.py:226
  31.6 0.4 feature_partials.1
  32.0 16.0 %all_to_all.11 = f32[32,2,128]{2,1,0:T(2,128)S(1)} all-to-all(f32[32,2,128]{2,1,0:T(2,128)S(1)} %bitcast.6), channel_id=1, replica_groups=mesh['zh'=2,'y'=4,'core'=2,'zl'=4,'x'=4] {'y','core','x'}, dimensions={0} | all-to-all | bytes 65536 | tf_op jit(solution)/shard_map/all_to_all | solution.py:235
  47.9 0.6 %reduce_sum.9 = f32[4,2,128]{2,1,0:T(2,128)} reduce(f32[8,4,2,128]{3,2,1,0:T(2,128)S(1)} %bitcast.8, f32[]{:T(128)} %constant.0.clone.1), dimensions={0}, to_apply=%region_0.0 | reduce | flops 7168 | bytes 36868 | tf_op jit(solution)/shard_map/reduce_sum | solution.py:238
  (4 shorter events, 0.0 us)
Async XLA Ops:
  0.0 1.5 %copy-start.2 = (s32[2]{0:T(128)S(1)}, s32[2]{0:T(128)}, u32[]{:S(2)}) copy-start(s32[2]{0:T(128)} %offsets.1) | copy-start | bytes 28
  0.0 1.5 %copy-start.1 = (s32[2]{0:T(128)S(1)}, s32[2]{0:T(128)}, u32[]{:S(2)}) copy-start(s32[2]{0:T(128)} %seeds.1) | copy-start | bytes 28
  0.0 1.5 %copy-start = (bf16[4,128,864]{1,2,0:T(8,128)(2,1)S(1)}, bf16[4,128,864]{1,2,0:T(8,128)(2,1)}, u32[]{:S(2)}) copy-start(bf16[4,128,864]{1,2,0:T(8,128)(2,1)} %param.5) | copy-start | bytes 2654212
  2.7 7.2 %collective-permute-start.3 = (f32[2,64,128]{2,1,0:T(8,128)S(1)}, f32[2,64,128]{2,1,0:T(8,128)S(1)}, u32[]{:S(2)}, u32[]{:S(2)}) collective-permute-start(f32[2,64,128]{2,1,0:T(8,128)S(1)} %get-tuple-element.17.after), channel_id=1, source_target_pairs={{0,1},{1,0},{2,3},{3,2},{4,5},{5,4},{6,7},{7,6},{8,9},{9,8},{10,11... | collective-permute-start | bytes 196616 | tf_op jit(solution)/shard_map/ppermute | solution.py:174
  4.8 2.1 %collective-permute-start = (f32[2,2,16,128]{3,2,1,0:T(8,128)S(1)}, f32[2,2,16,128]{3,2,1,0:T(8,128)S(1)}, u32[]{:S(2)}, u32[]{:S(2)}) collective-permute-start(f32[2,2,16,128]{3,2,1,0:T(8,128)S(1)} %get-tuple-element.16.after), channel_id=1, source_target_pairs={{0,16},{16,0},{1,17},{17,1},{2,18},{18,2},{3,19},{19,3},{4,20},{20... | collective-permute-start | bytes 98312 | tf_op jit(solution)/shard_map/ppermute | solution.py:174
  6.9 2.9 %collective-permute-start.1 = (f32[2,16,128]{2,1,0:T(8,128)S(1)}, f32[2,16,128]{2,1,0:T(8,128)S(1)}, u32[]{:S(2)}, u32[]{:S(2)}) collective-permute-start(f32[2,16,128]{2,1,0:T(8,128)S(1)} %get-tuple-element.19), channel_id=1, source_target_pairs={{0,32},{32,0},{64,96},{96,64},{1,33},{33,1},{65,97},{97,65},{2,34}... | collective-permute-start | bytes 49160 | tf_op jit(solution)/shard_map/ppermute | solution.py:174
  9.8 5.1 %collective-permute-start.4 = (f32[64,128]{1,0:T(8,128)S(1)}, f32[64,128]{1,0:T(8,128)S(1)}, u32[]{:S(2)}, u32[]{:S(2)}) collective-permute-start(f32[64,128]{1,0:T(8,128)S(1)} %get-tuple-element.24), channel_id=1, source_target_pairs={{0,3},{1,2},{2,1},{3,0},{4,7},{5,6},{6,5},{7,4},{8,11},{9,10},{10,... | collective-permute-start | bytes 98312 | tf_op jit(solution)/shard_map/ppermute | solution.py:174
  11.1 3.8 %collective-permute-start.2 = (f32[16,128]{1,0:T(8,128)S(1)}, f32[16,128]{1,0:T(8,128)S(1)}, u32[]{:S(2)}, u32[]{:S(2)}) collective-permute-start(f32[16,128]{1,0:T(8,128)S(1)} %get-tuple-element.21.after), channel_id=1, source_target_pairs={{0,96},{32,64},{64,32},{96,0},{1,97},{33,65},{65,33},{97,1},{2,98}... | collective-permute-start | bytes 24584 | tf_op jit(solution)/shard_map/ppermute | solution.py:174

commit v4 on v3

--- a/solution.py
+++ b/solution.py
@@ -120,6 +120,11 @@
     send[...] = own[1] + got[1]
 
 
+def add_through_kernel(own, got, passed, send, keep, handed_on):
+    keep[...] = own[0] + got[0]
+    send[...] = own[1] + got[1]
+
+
 def pack_kernel(in_own, in_got, out_own, out_got, packed):
     side_in = in_own[...] + in_got[...]
     side_out = out_own[...] + out_got[...]
@@ -208,7 +213,15 @@
         compiler_params=params,
         name="output_terms",
     )(hash_seeds, offsets, grads, in_send)
-    in_send, in_keep = add(in_keep, in_got, out_send, "add_core")
+    in_send, in_keep, out_send = pl.pallas_call(
+        add_through_kernel,
+        out_shape=[shaped(2, IN_SENT, LANES)] * 2 + [shaped(2, K_OUT, LANES)],
+        in_specs=[vmem, vmem, anywhere],
+        out_specs=[vmem, vmem, anywhere],
+        input_output_aliases={2: 2},
+        compiler_params=params,
+        name="add_core",
+    )(in_keep, in_got, out_send)
     in_got = swap(in_send, "y", 1)
     out_got = swap(out_send, "x", 1)
     in_send, in_keep = add(in_keep, in_got, in_got, "add_y")

time: 48.7 us -> 47.6 us (0.977)
  starting transfers between devices: 8.4 us -> 7.77 us
  blocking collectives: 32.6 us -> 32 us
    ppermute x5, starting transfers between devices: 8.4 us -> 7.77 us  [swap(): return lax.ppermute(value, axis, [(i, i ^ distance) for i in range(size)])]
  transfers between devices with their start and end apart: 5 -> 5, of which waited for: 3 -> 3; matrix products, arithmetic and copies ran while one was open for 0% -> 0% of each run, Pallas kernels for 0% -> 2%
where the time goes in v4:
time: 47.6 us; the launch traced here: 47.4 us
  blocking collectives  32 us (67%)
  starting transfers between devices  7.77 us (16%)
  waiting for transfers between devices  3.93 us (8%)
  Pallas kernels  3.02 us (6%)
  other arithmetic  0.62 us (1%)
    all_to_all x1, blocking collectives, body(): packed = lax.all_to_all(packed, ('zh', 'zl'), 0, 0, tiled=True)  16.4 us
    all_to_all x1, blocking collectives, body(): lax.all_to_all(spread.reshape(32, 2, LANES), ('y', 'core', 'x'), 0, 0, ti...  15.6 us
    ppermute x5, starting transfers between devices, swap(): return lax.ppermute(value, axis, [(i, i ^ distance) for i in range(size)])  7.77 us
    ppermute x5, waiting for transfers between devices, swap(): return lax.ppermute(value, axis, [(i, i ^ distance) for i in range(size)])  3.93 us
    pallas_call x1, Pallas kernels, body(): pl.pallas_call(input_kernel, out_shape=[shaped(2, 2, IN_SENT, LANES)] * 2...  1.43 us
    pallas_call x1, Pallas kernels, body(): pl.pallas_call(output_kernel, out_shape=[shaped(2, K_OUT, LANES)] * 2, in...  1.17 us
  transfers between devices with their start and end apart: 5, of which 3 were waited for; matrix products, arithmetic and copies ran while one was open for 0% of the time, Pallas kernels for 2%

profile of v4, /device:TPU:1, one launch (start us, length us, event | category | flops | bytes accessed | tf_op | source)
XLA Modules:
  0.0 47.4 jit_solution(14128222350413081326)
XLA Ops:
  0.0 0.0 copy-start.2
  0.0 0.0 copy-start.1
  0.0 0.0 copy-start
  0.0 1.4 %input_terms.1 = (f32[2,2,16,128]{3,2,1,0:T(8,128)S(1)}, f32[2,2,16,128]{3,2,1,0:T(8,128)S(1)}) custom-call(s32[2]{0:T(128)} %seeds.1, s32[2]{0:T(128)} %offsets.1, bf16[4,320,2048]{2,1,0:T(8,128)(2,1)} %bitcast.7), custom_call_target="tpu_custom_call" | custom-call | tf_op jit(solution)/shard_map/input_terms/pallas_call | solution.py:191
  1.5 3.3 %collective-permute-start = (f32[2,2,16,128]{3,2,1,0:T(8,128)S(1)}, f32[2,2,16,128]{3,2,1,0:T(8,128)S(1)}, u32[]{:S(2)}, u32[]{:S(2)}) collective-permute-start(f32[2,2,16,128]{3,2,1,0:T(8,128)S(1)} %get-tuple-element.17.after), channel_id=1, source_target_pairs={{0,16},{16,0},{1,17},{17,1},{2,18},{18,2},{3,19},{19,3},{4,20},{20... | collective-permute-start | bytes 98312 | tf_op jit(solution)/shard_map/ppermute | solution.py:179
  4.8 0.0 copy-done.2
  4.8 0.0 copy-done.1
  4.8 0.0 copy-done
  4.8 1.2 %output_terms.1 = (f32[2,64,128]{2,1,0:T(8,128)S(1)}, f32[2,64,128]{2,1,0:T(8,128)S(1)}) custom-call(s32[2]{0:T(128)S(1)} %copy-done.1, s32[2]{0:T(128)S(1)} %copy-done.2, bf16[4,864,128]{2,1,0:T(8,128)(2,1)S(1)} %bitcast.5, f32[2,2,16,128]{3,2,1,0:T(8,128)S(1)} %get-tuple-element.17.after), custom_call_target="tpu_custom_call" | custom-call | tf_op jit(solution)/shard_map/output_terms/pallas_call | solution.py:208
  5.9 0.0 collective-permute-done.got
  6.0 0.1 collective-permute-start.3
  6.1 0.8 %collective-permute-start.1 = (f32[2,16,128]{2,1,0:T(8,128)S(1)}, f32[2,16,128]{2,1,0:T(8,128)S(1)}, u32[]{:S(2)}, u32[]{:S(2)}) collective-permute-start(f32[2,16,128]{2,1,0:T(8,128)S(1)} %get-tuple-element.20), channel_id=1, source_target_pairs={{0,32},{32,0},{64,96},{96,64},{1,33},{33,1},{65,97},{97,65},{2,34}... | collective-permute-start | bytes 49160 | tf_op jit(solution)/shard_map/ppermute | solution.py:179
  6.8 1.9 %collective-permute-done.1.got.after = f32[2,16,128]{2,1,0:T(8,128)S(1)} collective-permute-done((f32[2,16,128]{2,1,0:T(8,128)S(1)}, f32[2,16,128]{2,1,0:T(8,128)S(1)}, u32[]{:S(2)}, u32[]{:S(2)}) %collective-permute-start.1) | collective-permute-done | bytes 16416 | tf_op jit(solution)/shard_map/ppermute | solution.py:179
  8.7 1.0 %collective-permute-done.3.got = f32[2,64,128]{2,1,0:T(8,128)S(1)} collective-permute-done((f32[2,64,128]{2,1,0:T(8,128)S(1)}, f32[2,64,128]{2,1,0:T(8,128)S(1)}, u32[]{:S(2)}, u32[]{:S(2)}) %collective-permute-start.3) | collective-permute-done | bytes 65568 | tf_op jit(solution)/shard_map/ppermute | solution.py:179
  9.8 0.9 %collective-permute-start.4 = (f32[64,128]{1,0:T(8,128)S(1)}, f32[64,128]{1,0:T(8,128)S(1)}, u32[]{:S(2)}, u32[]{:S(2)}) collective-permute-start(f32[64,128]{1,0:T(8,128)S(1)} %get-tuple-element.26), channel_id=1, source_target_pairs={{0,3},{1,2},{2,1},{3,0},{4,7},{5,6},{6,5},{7,4},{8,11},{9,10},{10,... | collective-permute-start | bytes 98312 | tf_op jit(solution)/shard_map/ppermute | solution.py:179
  10.6 2.7 %collective-permute-start.2 = (f32[16,128]{1,0:T(8,128)S(1)}, f32[16,128]{1,0:T(8,128)S(1)}, u32[]{:S(2)}, u32[]{:S(2)}) collective-permute-start(f32[16,128]{1,0:T(8,128)S(1)} %get-tuple-element.22.after), channel_id=1, source_target_pairs={{0,96},{32,64},{64,32},{96,0},{1,97},{33,65},{65,33},{97,1},{2,98}... | collective-permute-start | bytes 24584 | tf_op jit(solution)/shard_map/ppermute | solution.py:179
  13.3 1.0 %collective-permute-done.2.in_got = f32[16,128]{1,0:T(8,128)S(1)} collective-permute-done((f32[16,128]{1,0:T(8,128)S(1)}, f32[16,128]{1,0:T(8,128)S(1)}, u32[]{:S(2)}, u32[]{:S(2)}) %collective-permute-start.2) | collective-permute-done | bytes 8224 | tf_op jit(solution)/shard_map/ppermute | solution.py:179
  14.4 0.0 collective-permute-done.4.out_got
  14.4 16.4 %all_to_all.10.packed = f32[8,40,128]{2,1,0:T(8,128)S(1)} all-to-all(f32[8,40,128]{2,1,0:T(8,128)S(1)} %pack_sides.1), channel_id=1, replica_groups=mesh['zh'=2,'y'=4,'core'=2,'zl'=4,'x'=4] {'zh','zl'}, dimensions={0} | all-to-all | bytes 327680 | tf_op jit(solution)/shard_map/all_to_all | solution.py:239
  30.8 0.4 feature_partials.1
  31.2 15.6 %all_to_all.11 = f32[32,2,128]{2,1,0:T(2,128)S(1)} all-to-all(f32[32,2,128]{2,1,0:T(2,128)S(1)} %bitcast.6), channel_id=1, replica_groups=mesh['zh'=2,'y'=4,'core'=2,'zl'=4,'x'=4] {'y','core','x'}, dimensions={0} | all-to-all | bytes 65536 | tf_op jit(solution)/shard_map/all_to_all | solution.py:248
  46.8 0.6 %reduce_sum.9 = f32[4,2,128]{2,1,0:T(2,128)} reduce(f32[8,4,2,128]{3,2,1,0:T(2,128)S(1)} %bitcast.8, f32[]{:T(128)} %constant.0.clone.1), dimensions={0}, to_apply=%region_0.0 | reduce | flops 7168 | bytes 36868 | tf_op jit(solution)/shard_map/reduce_sum | solution.py:251
  (4 shorter events, 0.0 us)
Async XLA Ops:
  0.0 4.8 %copy-start.2 = (s32[2]{0:T(128)S(1)}, s32[2]{0:T(128)}, u32[]{:S(2)}) copy-start(s32[2]{0:T(128)} %offsets.1) | copy-start | bytes 28
  0.0 4.8 %copy-start.1 = (s32[2]{0:T(128)S(1)}, s32[2]{0:T(128)}, u32[]{:S(2)}) copy-start(s32[2]{0:T(128)} %seeds.1) | copy-start | bytes 28
  0.0 4.8 %copy-start = (bf16[4,128,864]{1,2,0:T(8,128)(2,1)S(1)}, bf16[4,128,864]{1,2,0:T(8,128)(2,1)}, u32[]{:S(2)}) copy-start(bf16[4,128,864]{1,2,0:T(8,128)(2,1)} %param.5) | copy-start | bytes 2654212
  1.5 4.5 %collective-permute-start = (f32[2,2,16,128]{3,2,1,0:T(8,128)S(1)}, f32[2,2,16,128]{3,2,1,0:T(8,128)S(1)}, u32[]{:S(2)}, u32[]{:S(2)}) collective-permute-start(f32[2,2,16,128]{3,2,1,0:T(8,128)S(1)} %get-tuple-element.17.after), channel_id=1, source_target_pairs={{0,16},{16,0},{1,17},{17,1},{2,18},{18,2},{3,19},{19,3},{4,20},{20... | collective-permute-start | bytes 98312 | tf_op jit(solution)/shard_map/ppermute | solution.py:179
  6.0 3.8 %collective-permute-start.3 = (f32[2,64,128]{2,1,0:T(8,128)S(1)}, f32[2,64,128]{2,1,0:T(8,128)S(1)}, u32[]{:S(2)}, u32[]{:S(2)}) collective-permute-start(f32[2,64,128]{2,1,0:T(8,128)S(1)} %get-tuple-element.24), channel_id=1, source_target_pairs={{0,1},{1,0},{2,3},{3,2},{4,5},{5,4},{6,7},{7,6},{8,9},{9,8},{10,11... | collective-permute-start | bytes 196616 | tf_op jit(solution)/shard_map/ppermute | solution.py:179
  6.1 2.7 %collective-permute-start.1 = (f32[2,16,128]{2,1,0:T(8,128)S(1)}, f32[2,16,128]{2,1,0:T(8,128)S(1)}, u32[]{:S(2)}, u32[]{:S(2)}) collective-permute-start(f32[2,16,128]{2,1,0:T(8,128)S(1)} %get-tuple-element.20), channel_id=1, source_target_pairs={{0,32},{32,0},{64,96},{96,64},{1,33},{33,1},{65,97},{97,65},{2,34}... | collective-permute-start | bytes 49160 | tf_op jit(solution)/shard_map/ppermute | solution.py:179
  9.8 4.6 %collective-permute-start.4 = (f32[64,128]{1,0:T(8,128)S(1)}, f32[64,128]{1,0:T(8,128)S(1)}, u32[]{:S(2)}, u32[]{:S(2)}) collective-permute-start(f32[64,128]{1,0:T(8,128)S(1)} %get-tuple-element.26), channel_id=1, source_target_pairs={{0,3},{1,2},{2,1},{3,0},{4,7},{5,6},{6,5},{7,4},{8,11},{9,10},{10,... | collective-permute-start | bytes 98312 | tf_op jit(solution)/shard_map/ppermute | solution.py:179
  10.6 3.8 %collective-permute-start.2 = (f32[16,128]{1,0:T(8,128)S(1)}, f32[16,128]{1,0:T(8,128)S(1)}, u32[]{:S(2)}, u32[]{:S(2)}) collective-permute-start(f32[16,128]{1,0:T(8,128)S(1)} %get-tuple-element.22.after), channel_id=1, source_target_pairs={{0,96},{32,64},{64,32},{96,0},{1,97},{33,65},{65,33},{97,1},{2,98}... | collective-permute-start | bytes 24584 | tf_op jit(solution)/shard_map/ppermute | solution.py:179

commit v5 on v4

--- a/solution.py
+++ b/solution.py
@@ -137,25 +137,35 @@
 
 def feature_kernel(packed, spread):
     factor_half = lax.shift_right_logical(lax.axis_index("zl"), 1)
-    total = None
+    sides_in, sides_out = [], []
     for z in range(2):
         source = z * 4
-        side_out = (packed[source, :OUT_HERE] + packed[source + 1, :OUT_HERE]) + (
-            packed[source + 2, :OUT_HERE] + packed[source + 3, :OUT_HERE]
+        sides_out.append(
+            (packed[source, :OUT_HERE] + packed[source + 1, :OUT_HERE])
+            + (packed[source + 2, :OUT_HERE] + packed[source + 3, :OUT_HERE])
         )
         source = z * 2 + factor_half
-        side_in = packed[source, OUT_HERE:] + packed[4 + source, OUT_HERE:]
-        product = lax.dot_general(
-            side_in,
-            jnp.concatenate([side_out] * 4, axis=0),
-            (((1,), (1,)), ((), ())),
-            precision=lax.Precision.HIGHEST,
-            preferred_element_type=jnp.float32,
-        )
-        total = product if total is None else total + product
-    total = total * SEQ_LEN ** (-0.5)
+        sides_in.append(packed[source, OUT_HERE:] + packed[4 + source, OUT_HERE:])
+    product = lax.dot_general(
+        jnp.concatenate(sides_in, axis=1) * SEQ_LEN ** (-0.5),
+        jnp.concatenate(sides_out, axis=1),
+        (((1,), (1,)), ((), ())),
+        precision=lax.Precision.HIGHEST,
+        preferred_element_type=jnp.float32,
+    )
+    total = jnp.concatenate(
+        [product, jnp.zeros((IN_HERE, LANES - OUT_HERE), jnp.float32)], axis=1
+    )
     for place in range(8):
         spread[place] = total if place == 0 else pltpu.roll(total, LANES - 4 * place, 1)
+
+
+def sum_kernel(parts, features):
+    total = parts[0]
+    for place in range(1, 8):
+        total = total + parts[place]
+    for seq in range(SEQS):
+        features[seq] = total[2 * seq : 2 * seq + 2, :4]
 
 
 def body(activations, out_grads, hash_seeds, offsets):

time: 47.6 us -> 47.4 us (level)
  no operation moved by 1% of the time
where the time goes in v5:
time: 47.4 us; the launch traced here: 47.3 us
  blocking collectives  32 us (68%)
  starting transfers between devices  7.77 us (16%)
  waiting for transfers between devices  3.93 us (8%)
  Pallas kernels  2.85 us (6%)
  other arithmetic  0.62 us (1%)
    all_to_all x1, blocking collectives, body(): packed = lax.all_to_all(packed, ('zh', 'zl'), 0, 0, tiled=True)  16.4 us
    all_to_all x1, blocking collectives, body(): lax.all_to_all(spread.reshape(32, 2, LANES), ('y', 'core', 'x'), 0, 0, ti...  15.6 us
    ppermute x5, starting transfers between devices, swap(): return lax.ppermute(value, axis, [(i, i ^ distance) for i in range(size)])  7.77 us
    ppermute x5, waiting for transfers between devices, swap(): return lax.ppermute(value, axis, [(i, i ^ distance) for i in range(size)])  3.93 us
    pallas_call x1, Pallas kernels, body(): pl.pallas_call(input_kernel, out_shape=[shaped(2, 2, IN_SENT, LANES)] * 2...  1.43 us
    pallas_call x1, Pallas kernels, body(): pl.pallas_call(output_kernel, out_shape=[shaped(2, K_OUT, LANES)] * 2, in...  1.17 us
  transfers between devices with their start and end apart: 5, of which 3 were waited for; matrix products, arithmetic and copies ran while one was open for 0% of the time, Pallas kernels for 2%

profile of v5, /device:TPU:1, one launch (start us, length us, event | category | flops | bytes accessed | tf_op | source)
XLA Modules:
  0.0 47.3 jit_solution(9952982300280495729)
XLA Ops:
  0.0 0.0 copy-start.2
  0.0 0.0 copy-start.1
  0.0 0.0 copy-start
  0.0 1.4 %input_terms.1 = (f32[2,2,16,128]{3,2,1,0:T(8,128)S(1)}, f32[2,2,16,128]{3,2,1,0:T(8,128)S(1)}) custom-call(s32[2]{0:T(128)} %seeds.1, s32[2]{0:T(128)} %offsets.1, bf16[4,320,2048]{2,1,0:T(8,128)(2,1)} %bitcast.7), custom_call_target="tpu_custom_call" | custom-call | tf_op jit(solution)/shard_map/input_terms/pallas_call | solution.py:201
  1.5 3.3 %collective-permute-start = (f32[2,2,16,128]{3,2,1,0:T(8,128)S(1)}, f32[2,2,16,128]{3,2,1,0:T(8,128)S(1)}, u32[]{:S(2)}, u32[]{:S(2)}) collective-permute-start(f32[2,2,16,128]{3,2,1,0:T(8,128)S(1)} %get-tuple-element.17.after), channel_id=1, source_target_pairs={{0,16},{16,0},{1,17},{17,1},{2,18},{18,2},{3,19},{19,3},{4,20},{20... | collective-permute-start | bytes 98312 | tf_op jit(solution)/shard_map/ppermute | solution.py:189
  4.8 0.0 copy-done.2
  4.8 0.0 copy-done.1
  4.8 0.0 copy-done
  4.8 1.2 %output_terms.1 = (f32[2,64,128]{2,1,0:T(8,128)S(1)}, f32[2,64,128]{2,1,0:T(8,128)S(1)}) custom-call(s32[2]{0:T(128)S(1)} %copy-done.1, s32[2]{0:T(128)S(1)} %copy-done.2, bf16[4,864,128]{2,1,0:T(8,128)(2,1)S(1)} %bitcast.5, f32[2,2,16,128]{3,2,1,0:T(8,128)S(1)} %get-tuple-element.17.after), custom_call_target="tpu_custom_call" | custom-call | tf_op jit(solution)/shard_map/output_terms/pallas_call | solution.py:218
  5.9 0.0 collective-permute-done.got
  6.0 0.1 collective-permute-start.3
  6.1 0.8 %collective-permute-start.1 = (f32[2,16,128]{2,1,0:T(8,128)S(1)}, f32[2,16,128]{2,1,0:T(8,128)S(1)}, u32[]{:S(2)}, u32[]{:S(2)}) collective-permute-start(f32[2,16,128]{2,1,0:T(8,128)S(1)} %get-tuple-element.20), channel_id=1, source_target_pairs={{0,32},{32,0},{64,96},{96,64},{1,33},{33,1},{65,97},{97,65},{2,34}... | collective-permute-start | bytes 49160 | tf_op jit(solution)/shard_map/ppermute | solution.py:189
  6.8 1.9 %collective-permute-done.1.got.after = f32[2,16,128]{2,1,0:T(8,128)S(1)} collective-permute-done((f32[2,16,128]{2,1,0:T(8,128)S(1)}, f32[2,16,128]{2,1,0:T(8,128)S(1)}, u32[]{:S(2)}, u32[]{:S(2)}) %collective-permute-start.1) | collective-permute-done | bytes 16416 | tf_op jit(solution)/shard_map/ppermute | solution.py:189
  8.7 1.0 %collective-permute-done.3.got = f32[2,64,128]{2,1,0:T(8,128)S(1)} collective-permute-done((f32[2,64,128]{2,1,0:T(8,128)S(1)}, f32[2,64,128]{2,1,0:T(8,128)S(1)}, u32[]{:S(2)}, u32[]{:S(2)}) %collective-permute-start.3) | collective-permute-done | bytes 65568 | tf_op jit(solution)/shard_map/ppermute | solution.py:189
  9.8 0.9 %collective-permute-start.4 = (f32[64,128]{1,0:T(8,128)S(1)}, f32[64,128]{1,0:T(8,128)S(1)}, u32[]{:S(2)}, u32[]{:S(2)}) collective-permute-start(f32[64,128]{1,0:T(8,128)S(1)} %get-tuple-element.26), channel_id=1, source_target_pairs={{0,3},{1,2},{2,1},{3,0},{4,7},{5,6},{6,5},{7,4},{8,11},{9,10},{10,... | collective-permute-start | bytes 98312 | tf_op jit(solution)/shard_map/ppermute | solution.py:189
  10.6 2.7 %collective-permute-start.2 = (f32[16,128]{1,0:T(8,128)S(1)}, f32[16,128]{1,0:T(8,128)S(1)}, u32[]{:S(2)}, u32[]{:S(2)}) collective-permute-start(f32[16,128]{1,0:T(8,128)S(1)} %get-tuple-element.22.after), channel_id=1, source_target_pairs={{0,96},{32,64},{64,32},{96,0},{1,97},{33,65},{65,33},{97,1},{2,98}... | collective-permute-start | bytes 24584 | tf_op jit(solution)/shard_map/ppermute | solution.py:189
  13.3 1.0 %collective-permute-done.2.in_got = f32[16,128]{1,0:T(8,128)S(1)} collective-permute-done((f32[16,128]{1,0:T(8,128)S(1)}, f32[16,128]{1,0:T(8,128)S(1)}, u32[]{:S(2)}, u32[]{:S(2)}) %collective-permute-start.2) | collective-permute-done | bytes 8224 | tf_op jit(solution)/shard_map/ppermute | solution.py:189
  14.4 0.0 collective-permute-done.4.out_got
  14.4 16.4 %all_to_all.10.packed = f32[8,40,128]{2,1,0:T(8,128)S(1)} all-to-all(f32[8,40,128]{2,1,0:T(8,128)S(1)} %pack_sides.1), channel_id=1, replica_groups=mesh['zh'=2,'y'=4,'core'=2,'zl'=4,'x'=4] {'zh','zl'}, dimensions={0} | all-to-all | bytes 327680 | tf_op jit(solution)/shard_map/all_to_all | solution.py:249
  30.8 0.2 feature_partials.1
  31.1 15.6 %all_to_all.11 = f32[32,2,128]{2,1,0:T(2,128)S(1)} all-to-all(f32[32,2,128]{2,1,0:T(2,128)S(1)} %bitcast.6), channel_id=1, replica_groups=mesh['zh'=2,'y'=4,'core'=2,'zl'=4,'x'=4] {'y','core','x'}, dimensions={0} | all-to-all | bytes 65536 | tf_op jit(solution)/shard_map/all_to_all | solution.py:258
  46.7 0.6 %reduce_sum.9 = f32[4,2,128]{2,1,0:T(2,128)} reduce(f32[8,4,2,128]{3,2,1,0:T(2,128)S(1)} %bitcast.8, f32[]{:T(128)} %constant.0.clone.1), dimensions={0}, to_apply=%region_0.0 | reduce | flops 7168 | bytes 36868 | tf_op jit(solution)/shard_map/reduce_sum | solution.py:261
  (4 shorter events, 0.0 us)
Async XLA Ops:
  0.0 4.8 %copy-start.2 = (s32[2]{0:T(128)S(1)}, s32[2]{0:T(128)}, u32[]{:S(2)}) copy-start(s32[2]{0:T(128)} %offsets.1) | copy-start | bytes 28
  0.0 4.8 %copy-start.1 = (s32[2]{0:T(128)S(1)}, s32[2]{0:T(128)}, u32[]{:S(2)}) copy-start(s32[2]{0:T(128)} %seeds.1) | copy-start | bytes 28
  0.0 4.8 %copy-start = (bf16[4,128,864]{1,2,0:T(8,128)(2,1)S(1)}, bf16[4,128,864]{1,2,0:T(8,128)(2,1)}, u32[]{:S(2)}) copy-start(bf16[4,128,864]{1,2,0:T(8,128)(2,1)} %param.5) | copy-start | bytes 2654212
  1.5 4.5 %collective-permute-start = (f32[2,2,16,128]{3,2,1,0:T(8,128)S(1)}, f32[2,2,16,128]{3,2,1,0:T(8,128)S(1)}, u32[]{:S(2)}, u32[]{:S(2)}) collective-permute-start(f32[2,2,16,128]{3,2,1,0:T(8,128)S(1)} %get-tuple-element.17.after), channel_id=1, source_target_pairs={{0,16},{16,0},{1,17},{17,1},{2,18},{18,2},{3,19},{19,3},{4,20},{20... | collective-permute-start | bytes 98312 | tf_op jit(solution)/shard_map/ppermute | solution.py:189
  6.0 3.8 %collective-permute-start.3 = (f32[2,64,128]{2,1,0:T(8,128)S(1)}, f32[2,64,128]{2,1,0:T(8,128)S(1)}, u32[]{:S(2)}, u32[]{:S(2)}) collective-permute-start(f32[2,64,128]{2,1,0:T(8,128)S(1)} %get-tuple-element.24), channel_id=1, source_target_pairs={{0,1},{1,0},{2,3},{3,2},{4,5},{5,4},{6,7},{7,6},{8,9},{9,8},{10,11... | collective-permute-start | bytes 196616 | tf_op jit(solution)/shard_map/ppermute | solution.py:189
  6.1 2.7 %collective-permute-start.1 = (f32[2,16,128]{2,1,0:T(8,128)S(1)}, f32[2,16,128]{2,1,0:T(8,128)S(1)}, u32[]{:S(2)}, u32[]{:S(2)}) collective-permute-start(f32[2,16,128]{2,1,0:T(8,128)S(1)} %get-tuple-element.20), channel_id=1, source_target_pairs={{0,32},{32,0},{64,96},{96,64},{1,33},{33,1},{65,97},{97,65},{2,34}... | collective-permute-start | bytes 49160 | tf_op jit(solution)/shard_map/ppermute | solution.py:189
  9.8 4.6 %collective-permute-start.4 = (f32[64,128]{1,0:T(8,128)S(1)}, f32[64,128]{1,0:T(8,128)S(1)}, u32[]{:S(2)}, u32[]{:S(2)}) collective-permute-start(f32[64,128]{1,0:T(8,128)S(1)} %get-tuple-element.26), channel_id=1, source_target_pairs={{0,3},{1,2},{2,1},{3,0},{4,7},{5,6},{6,5},{7,4},{8,11},{9,10},{10,... | collective-permute-start | bytes 98312 | tf_op jit(solution)/shard_map/ppermute | solution.py:189
  10.6 3.8 %collective-permute-start.2 = (f32[16,128]{1,0:T(8,128)S(1)}, f32[16,128]{1,0:T(8,128)S(1)}, u32[]{:S(2)}, u32[]{:S(2)}) collective-permute-start(f32[16,128]{1,0:T(8,128)S(1)} %get-tuple-element.22.after), channel_id=1, source_target_pairs={{0,96},{32,64},{64,32},{96,0},{1,97},{33,65},{65,33},{97,1},{2,98}... | collective-permute-start | bytes 24584 | tf_op jit(solution)/shard_map/ppermute | solution.py:189

commit v6 on v5

--- a/solution.py
+++ b/solution.py
@@ -15,6 +15,7 @@
 BLOCKS = SEQ_LEN // LANES
 IN_HERE = 8
 IN_SENT = 16
+SENT_ROWS = 40
 PARTS = 2
 PART = SEQ_LEN // 2 // PARTS
 OUT_HERE = 32
@@ -62,7 +63,7 @@
 
 
 def input_kernel(
-    seeds_hbm, offsets_hbm, acts, send, keep, seeds, offsets, held, blocks, arrived, told
+    seeds_hbm, offsets_hbm, acts, send, keep, out_table, seeds, offsets, held, blocks, arrived, told
 ):
     zh, y, core, zl, x = (lax.axis_index(axis) for axis in AXES)
     here = acts.shape[1]
@@ -88,6 +89,10 @@
     row = (zh * 4 + y) * 2 + core
     feature = row * here + lax.broadcasted_iota(jnp.int32, shape, 1)
     table = normal_draw(offsets[0] + feature * K_IN + factor, seeds[0], D)
+    shape = out_table.shape
+    factor = lax.broadcasted_iota(jnp.int32, shape, 0)
+    feature = (zl * 4 + x) * shape[1] + lax.broadcasted_iota(jnp.int32, shape, 1)
+    out_table[...] = normal_draw(offsets[1] + feature * K_OUT + factor, seeds[1], FF)
     for part in range(PARTS):
         fetches[part].wait()
         product = jnp.dot(table, held[part], preferred_element_type=jnp.float32)
@@ -98,20 +103,16 @@
     for out, other in ((send, core ^ 1), (keep, core)):
         for b in range(2):
             for c in range(2):
-                out[b, c] = blocks[(y ^ b ^ (3 * c)) * 2 + other]
-
-
-def output_kernel(seeds, offsets, grads, after, send, keep):
-    zl, x = (lax.axis_index(axis) for axis in COL)
-    here = grads.shape[1]
-    shape = (K_OUT, here)
-    factor = lax.broadcasted_iota(jnp.int32, shape, 0)
-    feature = (zl * 4 + x) * here + lax.broadcasted_iota(jnp.int32, shape, 1)
-    table = normal_draw(offsets[1] + feature * K_OUT + factor, seeds[1], FF)
+                out[b, c, :IN_SENT] = blocks[(y ^ b ^ (3 * c)) * 2 + other]
+    send[:, :, IN_SENT:] = jnp.zeros((2, 2, SENT_ROWS - IN_SENT, LANES), jnp.float32)
+
+
+def output_kernel(table, grads, send, keep):
+    x = lax.axis_index("x")
     for b, out in ((1, send), (0, keep)):
         for c in range(2):
             out[c] = jnp.dot(
-                table, grads[x ^ b ^ (3 * c)], preferred_element_type=jnp.float32
+                table[...], grads[x ^ b ^ (3 * c)], preferred_element_type=jnp.float32
             )
 
 
@@ -120,9 +121,9 @@
     send[...] = own[1] + got[1]
 
 
-def add_through_kernel(own, got, passed, send, keep, handed_on):
-    keep[...] = own[0] + got[0]
-    send[...] = own[1] + got[1]
+def add_core_kernel(own, got, send, keep):
+    keep[...] = own[0] + got[0, :, :IN_SENT]
+    send[...] = own[1] + got[1, :, :IN_SENT]
 
 
 def pack_kernel(in_own, in_got, out_own, out_got, packed):
@@ -172,7 +173,6 @@
     acts = jnp.swapaxes(activations, 1, 2)
     grads = jnp.swapaxes(out_grads, 1, 2)
     here_in = acts.shape[1]
-    smem = pl.BlockSpec(memory_space=pltpu.SMEM)
     vmem = pl.BlockSpec(memory_space=pltpu.VMEM)
     hbm = pl.BlockSpec(memory_space=pltpu.HBM)
     anywhere = pl.BlockSpec(memory_space=pl.ANY)
@@ -198,11 +198,12 @@
             name=name,
         )(own, got, after)
 
-    in_send, in_keep = pl.pallas_call(
+    in_send, in_keep, out_table = pl.pallas_call(
         input_kernel,
-        out_shape=[shaped(2, 2, IN_SENT, LANES)] * 2,
+        out_shape=[shaped(2, 2, SENT_ROWS, LANES), shaped(2, 2, IN_SENT, LANES)]
+        + [jax.ShapeDtypeStruct((K_OUT, grads.shape[1]), jnp.bfloat16)],
         in_specs=[hbm] * 3,
-        out_specs=[vmem] * 2,
+        out_specs=[vmem] * 3,
         scratch_shapes=[
             pltpu.SMEM((2,), jnp.int32),
             pltpu.SMEM((2,), jnp.int32),
@@ -218,20 +219,19 @@
     out_send, out_keep = pl.pallas_call(
         output_kernel,
         out_shape=[shaped(2, K_OUT, LANES)] * 2,
-        in_specs=[smem, smem, vmem, anywhere],
+        in_specs=[vmem] * 2,
         out_specs=[vmem] * 2,
         compiler_params=params,
         name="output_terms",
-    )(hash_seeds, offsets, grads, in_send)
-    in_send, in_keep, out_send = pl.pallas_call(
-        add_through_kernel,
-        out_shape=[shaped(2, IN_SENT, LANES)] * 2 + [shaped(2, K_OUT, LANES)],
-        in_specs=[vmem, vmem, anywhere],
-        out_specs=[vmem, vmem, anywhere],
-        input_output_aliases={2: 2},
+    )(out_table, grads)
+    in_send, in_keep = pl.pallas_call(
+        add_core_kernel,
+        out_shape=[shaped(2, IN_SENT, LANES)] * 2,
+        in_specs=[vmem] * 2,
+        out_specs=[vmem] * 2,
         compiler_params=params,
         name="add_core",
-    )(in_keep, in_got, out_send)
+    )(in_keep, in_got)
     in_got = swap(in_send, "y", 1)
     out_got = swap(out_send, "x", 1)
     in_send, in_keep = add(in_keep, in_got, in_got, "add_y")

time: 47.4 us -> 46.8 us (0.987)
  Pallas kernels: 2.85 us -> 2.15 us
    pallas_call x1, Pallas kernels: 1.17 us -> 0.3 us  [body(): pl.pallas_call(output_kernel, out_shape=[shaped(2, K_OUT, LANES)] * 2, in...]
  transfers between devices with their start and end apart: 5 -> 5, of which waited for: 3 -> 4; matrix products, arithmetic and copies ran while one was open for 0% -> 0% of each run, Pallas kernels for 2% -> 1%
where the time goes in v6:
time: 46.8 us; the launch traced here: 46.6 us
  blocking collectives  32.1 us (69%)
  starting transfers between devices  7.32 us (16%)
  waiting for transfers between devices  4.38 us (9%)
  Pallas kernels  2.15 us (5%)
  other arithmetic  0.62 us (1%)
    all_to_all x1, blocking collectives, body(): packed = lax.all_to_all(packed, ('zh', 'zl'), 0, 0, tiled=True)  16.5 us
    all_to_all x1, blocking collectives, body(): lax.all_to_all(spread.reshape(32, 2, LANES), ('y', 'core', 'x'), 0, 0, ti...  15.6 us
    ppermute x5, starting transfers between devices, swap(): return lax.ppermute(value, axis, [(i, i ^ distance) for i in range(size)])  7.32 us
    ppermute x5, waiting for transfers between devices, swap(): return lax.ppermute(value, axis, [(i, i ^ distance) for i in range(size)])  4.38 us
    pallas_call x1, Pallas kernels, body(): pl.pallas_call(input_kernel, out_shape=[shaped(2, 2, SENT_ROWS, LANES), s...  1.6 us
  transfers between devices with their start and end apart: 5, of which 4 were waited for; matrix products, arithmetic and copies ran while one was open for 0% of the time, Pallas kernels for 1%

profile of v6, /device:TPU:1, one launch (start us, length us, event | category | flops | bytes accessed | tf_op | source)
XLA Modules:
  0.0 46.6 jit_solution(6763877834529581923)
XLA Ops:
  0.0 0.0 copy-start
  0.0 1.6 %input_terms.1 = (f32[2,2,40,128]{3,2,1,0:T(8,128)S(1)}, f32[2,2,16,128]{3,2,1,0:T(8,128)S(1)}, bf16[64,864]{1,0:T(8,128)(2,1)S(1)}) custom-call(s32[2]{0:T(128)} %seeds_hbm.1, s32[2]{0:T(128)} %offsets_hbm.1, bf16[4,320,2048]{2,1,0:T(8,128)(2,1)} %bitcast.7), custom_call_target="tpu_custom_call" | custom-call | tf_op jit(solution)/shard_map/input_terms/pallas_call | solution.py:201
  1.6 3.3 %collective-permute-start = (f32[2,2,40,128]{3,2,1,0:T(8,128)S(1)}, f32[2,2,40,128]{3,2,1,0:T(8,128)S(1)}, u32[]{:S(2)}, u32[]{:S(2)}) collective-permute-start(f32[2,2,40,128]{3,2,1,0:T(8,128)S(1)} %get-tuple-element.17), channel_id=1, source_target_pairs={{0,16},{16,0},{1,17},{17,1},{2,18},{18,2},{3,19},{19,3},{4,20},{20... | collective-permute-start | bytes 245768 | tf_op jit(solution)/shard_map/ppermute | solution.py:189
  4.9 0.0 copy-done
  4.9 0.3 output_terms.1
  5.2 0.1 collective-permute-start.3
  5.4 0.5 %collective-permute-done.got = f32[2,2,40,128]{3,2,1,0:T(8,128)S(1)} collective-permute-done((f32[2,2,40,128]{3,2,1,0:T(8,128)S(1)}, f32[2,2,40,128]{3,2,1,0:T(8,128)S(1)}, u32[]{:S(2)}, u32[]{:S(2)}) %collective-permute-start) | collective-permute-done | bytes 81952 | tf_op jit(solution)/shard_map/ppermute | solution.py:189
  5.9 0.3 collective-permute-start.1
  6.2 2.5 %collective-permute-done.1.got.after = f32[2,16,128]{2,1,0:T(8,128)S(1)} collective-permute-done((f32[2,16,128]{2,1,0:T(8,128)S(1)}, f32[2,16,128]{2,1,0:T(8,128)S(1)}, u32[]{:S(2)}, u32[]{:S(2)}) %collective-permute-start.1) | collective-permute-done | bytes 16416 | tf_op jit(solution)/shard_map/ppermute | solution.py:189
  8.8 0.3 collective-permute-done.3.got
  9.1 0.8 %collective-permute-start.4 = (f32[64,128]{1,0:T(8,128)S(1)}, f32[64,128]{1,0:T(8,128)S(1)}, u32[]{:S(2)}, u32[]{:S(2)}) collective-permute-start(f32[64,128]{1,0:T(8,128)S(1)} %get-tuple-element.26), channel_id=1, source_target_pairs={{0,3},{1,2},{2,1},{3,0},{4,7},{5,6},{6,5},{7,4},{8,11},{9,10},{10,... | collective-permute-start | bytes 98312 | tf_op jit(solution)/shard_map/ppermute | solution.py:189
  9.9 2.7 %collective-permute-start.2 = (f32[16,128]{1,0:T(8,128)S(1)}, f32[16,128]{1,0:T(8,128)S(1)}, u32[]{:S(2)}, u32[]{:S(2)}) collective-permute-start(f32[16,128]{1,0:T(8,128)S(1)} %get-tuple-element.21.after), channel_id=1, source_target_pairs={{0,96},{32,64},{64,32},{96,0},{1,97},{33,65},{65,33},{97,1},{2,98}... | collective-permute-start | bytes 24584 | tf_op jit(solution)/shard_map/ppermute | solution.py:189
  12.6 1.0 %collective-permute-done.2.in_got = f32[16,128]{1,0:T(8,128)S(1)} collective-permute-done((f32[16,128]{1,0:T(8,128)S(1)}, f32[16,128]{1,0:T(8,128)S(1)}, u32[]{:S(2)}, u32[]{:S(2)}) %collective-permute-start.2) | collective-permute-done | bytes 8224 | tf_op jit(solution)/shard_map/ppermute | solution.py:189
  13.7 0.0 collective-permute-done.4.out_got
  13.7 16.5 %all_to_all.10.packed = f32[8,40,128]{2,1,0:T(8,128)S(1)} all-to-all(f32[8,40,128]{2,1,0:T(8,128)S(1)} %pack_sides.1), channel_id=1, replica_groups=mesh['zh'=2,'y'=4,'core'=2,'zl'=4,'x'=4] {'zh','zl'}, dimensions={0} | all-to-all | bytes 327680 | tf_op jit(solution)/shard_map/all_to_all | solution.py:249
  30.2 0.2 feature_partials.1
  30.4 15.6 %all_to_all.11 = f32[32,2,128]{2,1,0:T(2,128)S(1)} all-to-all(f32[32,2,128]{2,1,0:T(2,128)S(1)} %bitcast.6), channel_id=1, replica_groups=mesh['zh'=2,'y'=4,'core'=2,'zl'=4,'x'=4] {'y','core','x'}, dimensions={0} | all-to-all | bytes 65536 | tf_op jit(solution)/shard_map/all_to_all | solution.py:258
  46.0 0.6 %reduce_sum.9 = f32[4,2,128]{2,1,0:T(2,128)} reduce(f32[8,4,2,128]{3,2,1,0:T(2,128)S(1)} %bitcast.8, f32[]{:T(128)} %constant.0.clone.1), dimensions={0}, to_apply=%region_0.0 | reduce | flops 7168 | bytes 36868 | tf_op jit(solution)/shard_map/reduce_sum | solution.py:261
  (4 shorter events, 0.0 us)
Async XLA Ops:
  0.0 4.9 %copy-start = (bf16[4,128,864]{1,2,0:T(8,128)(2,1)S(1)}, bf16[4,128,864]{1,2,0:T(8,128)(2,1)}, u32[]{:S(2)}) copy-start(bf16[4,128,864]{1,2,0:T(8,128)(2,1)} %param.5) | copy-start | bytes 2654212
  1.6 4.3 %collective-permute-start = (f32[2,2,40,128]{3,2,1,0:T(8,128)S(1)}, f32[2,2,40,128]{3,2,1,0:T(8,128)S(1)}, u32[]{:S(2)}, u32[]{:S(2)}) collective-permute-start(f32[2,2,40,128]{3,2,1,0:T(8,128)S(1)} %get-tuple-element.17), channel_id=1, source_target_pairs={{0,16},{16,0},{1,17},{17,1},{2,18},{18,2},{3,19},{19,3},{4,20},{20... | collective-permute-start | bytes 245768 | tf_op jit(solution)/shard_map/ppermute | solution.py:189
  5.2 3.8 %collective-permute-start.3 = (f32[2,64,128]{2,1,0:T(8,128)S(1)}, f32[2,64,128]{2,1,0:T(8,128)S(1)}, u32[]{:S(2)}, u32[]{:S(2)}) collective-permute-start(f32[2,64,128]{2,1,0:T(8,128)S(1)} %get-tuple-element.24), channel_id=1, source_target_pairs={{0,1},{1,0},{2,3},{3,2},{4,5},{5,4},{6,7},{7,6},{8,9},{9,8},{10,11... | collective-permute-start | bytes 196616 | tf_op jit(solution)/shard_map/ppermute | solution.py:189
  5.9 2.9 %collective-permute-start.1 = (f32[2,16,128]{2,1,0:T(8,128)S(1)}, f32[2,16,128]{2,1,0:T(8,128)S(1)}, u32[]{:S(2)}, u32[]{:S(2)}) collective-permute-start(f32[2,16,128]{2,1,0:T(8,128)S(1)} %get-tuple-element.19), channel_id=1, source_target_pairs={{0,32},{32,0},{64,96},{96,64},{1,33},{33,1},{65,97},{97,65},{2,34}... | collective-permute-start | bytes 49160 | tf_op jit(solution)/shard_map/ppermute | solution.py:189
  9.1 4.6 %collective-permute-start.4 = (f32[64,128]{1,0:T(8,128)S(1)}, f32[64,128]{1,0:T(8,128)S(1)}, u32[]{:S(2)}, u32[]{:S(2)}) collective-permute-start(f32[64,128]{1,0:T(8,128)S(1)} %get-tuple-element.26), channel_id=1, source_target_pairs={{0,3},{1,2},{2,1},{3,0},{4,7},{5,6},{6,5},{7,4},{8,11},{9,10},{10,... | collective-permute-start | bytes 98312 | tf_op jit(solution)/shard_map/ppermute | solution.py:189
  9.9 3.8 %collective-permute-start.2 = (f32[16,128]{1,0:T(8,128)S(1)}, f32[16,128]{1,0:T(8,128)S(1)}, u32[]{:S(2)}, u32[]{:S(2)}) collective-permute-start(f32[16,128]{1,0:T(8,128)S(1)} %get-tuple-element.21.after), channel_id=1, source_target_pairs={{0,96},{32,64},{64,32},{96,0},{1,97},{33,65},{65,33},{97,1},{2,98}... | collective-permute-start | bytes 24584 | tf_op jit(solution)/shard_map/ppermute | solution.py:189

commit v7 on v6

--- a/solution.py
+++ b/solution.py
@@ -16,6 +16,7 @@
 IN_HERE = 8
 IN_SENT = 16
 SENT_ROWS = 40
+PADDED_ROWS = 36
 PARTS = 2
 PART = SEQ_LEN // 2 // PARTS
 OUT_HERE = 32
@@ -103,7 +104,7 @@
     for out, other in ((send, core ^ 1), (keep, core)):
         for b in range(2):
             for c in range(2):
-                out[b, c, :IN_SENT] = blocks[(y ^ b ^ (3 * c)) * 2 + other]
+                out[b, c, :IN_SENT] = blocks[(y ^ (3 * b) ^ c) * 2 + other]
     send[:, :, IN_SENT:] = jnp.zeros((2, 2, SENT_ROWS - IN_SENT, LANES), jnp.float32)
 
 
@@ -123,7 +124,13 @@
 
 def add_core_kernel(own, got, send, keep):
     keep[...] = own[0] + got[0, :, :IN_SENT]
-    send[...] = own[1] + got[1, :, :IN_SENT]
+    send[:, :IN_SENT] = own[1] + got[1, :, :IN_SENT]
+    send[:, IN_SENT:] = jnp.zeros((2, PADDED_ROWS - IN_SENT, LANES), jnp.float32)
+
+
+def add_y_kernel(own, got, after, send, keep):
+    keep[...] = own[0] + got[0, :IN_SENT]
+    send[...] = own[1] + got[1, :IN_SENT]
 
 
 def pack_kernel(in_own, in_got, out_own, out_got, packed):
@@ -226,18 +233,25 @@
     )(out_table, grads)
     in_send, in_keep = pl.pallas_call(
         add_core_kernel,
-        out_shape=[shaped(2, IN_SENT, LANES)] * 2,
+        out_shape=[shaped(2, PADDED_ROWS, LANES), shaped(2, IN_SENT, LANES)],
         in_specs=[vmem] * 2,
         out_specs=[vmem] * 2,
         compiler_params=params,
         name="add_core",
     )(in_keep, in_got)
-    in_got = swap(in_send, "y", 1)
+    in_got = swap(in_send, "y", 3)
     out_got = swap(out_send, "x", 1)
-    in_send, in_keep = add(in_keep, in_got, in_got, "add_y")
-    in_got = swap(in_send, "y", 3)
     out_send, out_keep = add(out_keep, out_got, in_send, "add_x")
     out_got = swap(out_send, "x", 3)
+    in_send, in_keep = pl.pallas_call(
+        add_y_kernel,
+        out_shape=[shaped(IN_SENT, LANES)] * 2,
+        in_specs=[vmem, vmem, anywhere],
+        out_specs=[vmem] * 2,
+        compiler_params=params,
+        name="add_y",
+    )(in_keep, in_got, out_send)
+    in_got = swap(in_send, "y", 1)
     packed = pl.pallas_call(
         pack_kernel,
         out_shape=shaped(8, OUT_HERE + IN_HERE, LANES),

time: 46.8 us -> 46.4 us (level)
  waiting for transfers between devices: 4.38 us -> 3.9 us
    all_to_all x1, blocking collectives: 15.6 us -> 16.4 us  [body(): lax.all_to_all(spread.reshape(32, 2, LANES), ('y', 'core', 'x'), 0, 0, ti...]
    all_to_all x1, blocking collectives: 16.5 us -> 15.9 us  [body(): packed = lax.all_to_all(packed, ('zh', 'zl'), 0, 0, tiled=True)]
    ppermute x5, waiting for transfers between devices: 4.38 us -> 3.9 us  [swap(): return lax.ppermute(value, axis, [(i, i ^ distance) for i in range(size)])]
where the time goes in v7:
time: 46.4 us; the launch traced here: 46.3 us
  blocking collectives  32.3 us (70%)
  starting transfers between devices  7.26 us (16%)
  waiting for transfers between devices  3.9 us (8%)
  Pallas kernels  2.15 us (5%)
  other arithmetic  0.62 us (1%)
    all_to_all x1, blocking collectives, body(): lax.all_to_all(spread.reshape(32, 2, LANES), ('y', 'core', 'x'), 0, 0, ti...  16.4 us
    all_to_all x1, blocking collectives, body(): packed = lax.all_to_all(packed, ('zh', 'zl'), 0, 0, tiled=True)  15.9 us
    ppermute x5, starting transfers between devices, swap(): return lax.ppermute(value, axis, [(i, i ^ distance) for i in range(size)])  7.26 us
    ppermute x5, waiting for transfers between devices, swap(): return lax.ppermute(value, axis, [(i, i ^ distance) for i in range(size)])  3.9 us
    pallas_call x1, Pallas kernels, body(): pl.pallas_call(input_kernel, out_shape=[shaped(2, 2, SENT_ROWS, LANES), s...  1.6 us
  transfers between devices with their start and end apart: 5, of which 4 were waited for; matrix products, arithmetic and copies ran while one was open for 0% of the time, Pallas kernels for 1%

profile of v7, /device:TPU:1, one launch (start us, length us, event | category | flops | bytes accessed | tf_op | source)
XLA Modules:
  0.0 46.3 jit_solution(4317109425284643812)
XLA Ops:
  0.0 0.0 copy-start
  0.0 1.6 %input_terms.1 = (f32[2,2,40,128]{3,2,1,0:T(8,128)S(1)}, f32[2,2,16,128]{3,2,1,0:T(8,128)S(1)}, bf16[64,864]{1,0:T(8,128)(2,1)S(1)}) custom-call(s32[2]{0:T(128)} %seeds_hbm.1, s32[2]{0:T(128)} %offsets_hbm.1, bf16[4,320,2048]{2,1,0:T(8,128)(2,1)} %bitcast.7), custom_call_target="tpu_custom_call" | custom-call | tf_op jit(solution)/shard_map/input_terms/pallas_call | solution.py:208
  1.6 3.3 %collective-permute-start = (f32[2,2,40,128]{3,2,1,0:T(8,128)S(1)}, f32[2,2,40,128]{3,2,1,0:T(8,128)S(1)}, u32[]{:S(2)}, u32[]{:S(2)}) collective-permute-start(f32[2,2,40,128]{3,2,1,0:T(8,128)S(1)} %get-tuple-element.17), channel_id=1, source_target_pairs={{0,16},{16,0},{1,17},{17,1},{2,18},{18,2},{3,19},{19,3},{4,20},{20... | collective-permute-start | bytes 245768 | tf_op jit(solution)/shard_map/ppermute | solution.py:196
  4.9 0.0 copy-done
  4.9 0.3 output_terms.1
  5.2 0.1 collective-permute-start.2
  5.3 0.5 %collective-permute-done.got = f32[2,2,40,128]{3,2,1,0:T(8,128)S(1)} collective-permute-done((f32[2,2,40,128]{3,2,1,0:T(8,128)S(1)}, f32[2,2,40,128]{3,2,1,0:T(8,128)S(1)}, u32[]{:S(2)}, u32[]{:S(2)}) %collective-permute-start) | collective-permute-done | bytes 81952 | tf_op jit(solution)/shard_map/ppermute | solution.py:196
  5.9 1.8 %collective-permute-start.1 = (f32[2,36,128]{2,1,0:T(8,128)S(1)}, f32[2,36,128]{2,1,0:T(8,128)S(1)}, u32[]{:S(2)}, u32[]{:S(2)}) collective-permute-start(f32[2,36,128]{2,1,0:T(8,128)S(1)} %get-tuple-element.19.after), channel_id=1, source_target_pairs={{0,96},{32,64},{64,32},{96,0},{1,97},{33,65},{65,33},{97,1},{2,98}... | collective-permute-start | bytes 110600 | tf_op jit(solution)/shard_map/ppermute | solution.py:196
  7.6 1.4 %collective-permute-done.2.got = f32[2,64,128]{2,1,0:T(8,128)S(1)} collective-permute-done((f32[2,64,128]{2,1,0:T(8,128)S(1)}, f32[2,64,128]{2,1,0:T(8,128)S(1)}, u32[]{:S(2)}, u32[]{:S(2)}) %collective-permute-start.2) | collective-permute-done | bytes 65568 | tf_op jit(solution)/shard_map/ppermute | solution.py:196
  9.1 0.8 %collective-permute-start.4 = (f32[64,128]{1,0:T(8,128)S(1)}, f32[64,128]{1,0:T(8,128)S(1)}, u32[]{:S(2)}, u32[]{:S(2)}) collective-permute-start(f32[64,128]{1,0:T(8,128)S(1)} %get-tuple-element.23.after), channel_id=1, source_target_pairs={{0,3},{1,2},{2,1},{3,0},{4,7},{5,6},{6,5},{7,4},{8,11},{9,10},{10,... | collective-permute-start | bytes 98312 | tf_op jit(solution)/shard_map/ppermute | solution.py:196
  9.9 0.1 collective-permute-done.1.got
  9.9 1.2 %collective-permute-start.3 = (f32[16,128]{1,0:T(8,128)S(1)}, f32[16,128]{1,0:T(8,128)S(1)}, u32[]{:S(2)}, u32[]{:S(2)}) collective-permute-start(f32[16,128]{1,0:T(8,128)S(1)} %get-tuple-element.25), channel_id=1, source_target_pairs={{0,32},{32,0},{64,96},{96,64},{1,33},{33,1},{65,97},{97,65},{2,34}... | collective-permute-start | bytes 24584 | tf_op jit(solution)/shard_map/ppermute | solution.py:196
  11.2 1.9 %collective-permute-done.4.out_got = f32[64,128]{1,0:T(8,128)S(1)} collective-permute-done((f32[64,128]{1,0:T(8,128)S(1)}, f32[64,128]{1,0:T(8,128)S(1)}, u32[]{:S(2)}, u32[]{:S(2)}) %collective-permute-start.4) | collective-permute-done | bytes 32800 | tf_op jit(solution)/shard_map/ppermute | solution.py:196
  13.1 0.0 collective-permute-done.3.in_got
  13.1 15.9 %all_to_all.10.packed = f32[8,40,128]{2,1,0:T(8,128)S(1)} all-to-all(f32[8,40,128]{2,1,0:T(8,128)S(1)} %pack_sides.1), channel_id=1, replica_groups=mesh['zh'=2,'y'=4,'core'=2,'zl'=4,'x'=4] {'zh','zl'}, dimensions={0} | all-to-all | bytes 327680 | tf_op jit(solution)/shard_map/all_to_all | solution.py:263
  29.1 0.2 feature_partials.1
  29.3 16.4 %all_to_all.11 = f32[32,2,128]{2,1,0:T(2,128)S(1)} all-to-all(f32[32,2,128]{2,1,0:T(2,128)S(1)} %bitcast.6), channel_id=1, replica_groups=mesh['zh'=2,'y'=4,'core'=2,'zl'=4,'x'=4] {'y','core','x'}, dimensions={0} | all-to-all | bytes 65536 | tf_op jit(solution)/shard_map/all_to_all | solution.py:272
  45.6 0.6 %reduce_sum.9 = f32[4,2,128]{2,1,0:T(2,128)} reduce(f32[8,4,2,128]{3,2,1,0:T(2,128)S(1)} %bitcast.8, f32[]{:T(128)} %constant.0.clone.1), dimensions={0}, to_apply=%region_0.0 | reduce | flops 7168 | bytes 36868 | tf_op jit(solution)/shard_map/reduce_sum | solution.py:275
  (4 shorter events, 0.0 us)
Async XLA Ops:
  0.0 4.9 %copy-start = (bf16[4,128,864]{1,2,0:T(8,128)(2,1)S(1)}, bf16[4,128,864]{1,2,0:T(8,128)(2,1)}, u32[]{:S(2)}) copy-start(bf16[4,128,864]{1,2,0:T(8,128)(2,1)} %param.5) | copy-start | bytes 2654212
  1.6 4.3 %collective-permute-start = (f32[2,2,40,128]{3,2,1,0:T(8,128)S(1)}, f32[2,2,40,128]{3,2,1,0:T(8,128)S(1)}, u32[]{:S(2)}, u32[]{:S(2)}) collective-permute-start(f32[2,2,40,128]{3,2,1,0:T(8,128)S(1)} %get-tuple-element.17), channel_id=1, source_target_pairs={{0,16},{16,0},{1,17},{17,1},{2,18},{18,2},{3,19},{19,3},{4,20},{20... | collective-permute-start | bytes 245768 | tf_op jit(solution)/shard_map/ppermute | solution.py:196
  5.2 3.8 %collective-permute-start.2 = (f32[2,64,128]{2,1,0:T(8,128)S(1)}, f32[2,64,128]{2,1,0:T(8,128)S(1)}, u32[]{:S(2)}, u32[]{:S(2)}) collective-permute-start(f32[2,64,128]{2,1,0:T(8,128)S(1)} %get-tuple-element.22), channel_id=1, source_target_pairs={{0,1},{1,0},{2,3},{3,2},{4,5},{5,4},{6,7},{7,6},{8,9},{9,8},{10,11... | collective-permute-start | bytes 196616 | tf_op jit(solution)/shard_map/ppermute | solution.py:196
  5.9 4.1 %collective-permute-start.1 = (f32[2,36,128]{2,1,0:T(8,128)S(1)}, f32[2,36,128]{2,1,0:T(8,128)S(1)}, u32[]{:S(2)}, u32[]{:S(2)}) collective-permute-start(f32[2,36,128]{2,1,0:T(8,128)S(1)} %get-tuple-element.19.after), channel_id=1, source_target_pairs={{0,96},{32,64},{64,32},{96,0},{1,97},{33,65},{65,33},{97,1},{2,98}... | collective-permute-start | bytes 110600 | tf_op jit(solution)/shard_map/ppermute | solution.py:196
  9.1 4.1 %collective-permute-start.4 = (f32[64,128]{1,0:T(8,128)S(1)}, f32[64,128]{1,0:T(8,128)S(1)}, u32[]{:S(2)}, u32[]{:S(2)}) collective-permute-start(f32[64,128]{1,0:T(8,128)S(1)} %get-tuple-element.23.after), channel_id=1, source_target_pairs={{0,3},{1,2},{2,1},{3,0},{4,7},{5,6},{6,5},{7,4},{8,11},{9,10},{10,... | collective-permute-start | bytes 98312 | tf_op jit(solution)/shard_map/ppermute | solution.py:196
  9.9 3.2 %collective-permute-start.3 = (f32[16,128]{1,0:T(8,128)S(1)}, f32[16,128]{1,0:T(8,128)S(1)}, u32[]{:S(2)}, u32[]{:S(2)}) collective-permute-start(f32[16,128]{1,0:T(8,128)S(1)} %get-tuple-element.25), channel_id=1, source_target_pairs={{0,32},{32,0},{64,96},{96,64},{1,33},{33,1},{65,97},{97,65},{2,34}... | collective-permute-start | bytes 24584 | tf_op jit(solution)/shard_map/ppermute | solution.py:196

commit v8 on v7

--- a/solution.py
+++ b/solution.py
@@ -137,9 +137,9 @@
     side_in = in_own[...] + in_got[...]
     side_out = out_own[...] + out_got[...]
     for dest in range(8):
-        half = (dest // 4) * OUT_HERE
+        half = (dest % 2) * OUT_HERE
         packed[dest, :OUT_HERE] = side_out[half : half + OUT_HERE]
-        half = (dest % 2) * IN_HERE
+        half = (dest // 2 % 2) * IN_HERE
         packed[dest, OUT_HERE:] = side_in[half : half + IN_HERE]
 
 
@@ -147,13 +147,12 @@
     factor_half = lax.shift_right_logical(lax.axis_index("zl"), 1)
     sides_in, sides_out = [], []
     for z in range(2):
-        source = z * 4
         sides_out.append(
-            (packed[source, :OUT_HERE] + packed[source + 1, :OUT_HERE])
-            + (packed[source + 2, :OUT_HERE] + packed[source + 3, :OUT_HERE])
+            (packed[z, :OUT_HERE] + packed[2 + z, :OUT_HERE])
+            + (packed[4 + z, :OUT_HERE] + packed[6 + z, :OUT_HERE])
         )
-        source = z * 2 + factor_half
-        sides_in.append(packed[source, OUT_HERE:] + packed[4 + source, OUT_HERE:])
+        source = (z * 2 + factor_half) * 2
+        sides_in.append(packed[source, OUT_HERE:] + packed[source + 1, OUT_HERE:])
     product = lax.dot_general(
         jnp.concatenate(sides_in, axis=1) * SEQ_LEN ** (-0.5),
         jnp.concatenate(sides_out, axis=1),
@@ -260,7 +259,7 @@
         compiler_params=params,
         name="pack_sides",
     )(in_keep, in_got, out_keep, out_got)
-    packed = lax.all_to_all(packed, ("zh", "zl"), 0, 0, tiled=True)
+    packed = lax.all_to_all(packed, ("zl", "zh"), 0, 0, tiled=True)
     spread = pl.pallas_call(
         feature_kernel,
         out_shape=shaped(8, 8, LANES),

time: 46.4 us -> 45.2 us (0.974)
  blocking collectives: 32.3 us -> 31 us
    all_to_all x1, blocking collectives: 15.9 us -> 14.4 us  [body(): packed = lax.all_to_all(packed, ('zl', 'zh'), 0, 0, tiled=True)]
where the time goes in v8:
time: 45.2 us; the launch traced here: 45 us
  blocking collectives  31 us (69%)
  starting transfers between devices  7.26 us (16%)
  waiting for transfers between devices  3.9 us (9%)
  Pallas kernels  2.15 us (5%)
  other arithmetic  0.62 us (1%)
    all_to_all x1, blocking collectives, body(): lax.all_to_all(spread.reshape(32, 2, LANES), ('y', 'core', 'x'), 0, 0, ti...  16.6 us
    all_to_all x1, blocking collectives, body(): packed = lax.all_to_all(packed, ('zl', 'zh'), 0, 0, tiled=True)  14.4 us
    ppermute x5, starting transfers between devices, swap(): return lax.ppermute(value, axis, [(i, i ^ distance) for i in range(size)])  7.26 us
    ppermute x5, waiting for transfers between devices, swap(): return lax.ppermute(value, axis, [(i, i ^ distance) for i in range(size)])  3.9 us
    pallas_call x1, Pallas kernels, body(): pl.pallas_call(input_kernel, out_shape=[shaped(2, 2, SENT_ROWS, LANES), s...  1.6 us
  transfers between devices with their start and end apart: 5, of which 4 were waited for; matrix products, arithmetic and copies ran while one was open for 0% of the time, Pallas kernels for 1%

profile of v8, /device:TPU:1, one launch (start us, length us, event | category | flops | bytes accessed | tf_op | source)
XLA Modules:
  0.0 45.0 jit_solution(18113029497666459554)
XLA Ops:
  0.0 0.0 copy-start
  0.0 1.6 %input_terms.1 = (f32[2,2,40,128]{3,2,1,0:T(8,128)S(1)}, f32[2,2,16,128]{3,2,1,0:T(8,128)S(1)}, bf16[64,864]{1,0:T(8,128)(2,1)S(1)}) custom-call(s32[2]{0:T(128)} %seeds_hbm.1, s32[2]{0:T(128)} %offsets_hbm.1, bf16[4,320,2048]{2,1,0:T(8,128)(2,1)} %bitcast.7), custom_call_target="tpu_custom_call" | custom-call | tf_op jit(solution)/shard_map/input_terms/pallas_call | solution.py:207
  1.6 3.3 %collective-permute-start = (f32[2,2,40,128]{3,2,1,0:T(8,128)S(1)}, f32[2,2,40,128]{3,2,1,0:T(8,128)S(1)}, u32[]{:S(2)}, u32[]{:S(2)}) collective-permute-start(f32[2,2,40,128]{3,2,1,0:T(8,128)S(1)} %get-tuple-element.17), channel_id=1, source_target_pairs={{0,16},{16,0},{1,17},{17,1},{2,18},{18,2},{3,19},{19,3},{4,20},{20... | collective-permute-start | bytes 245768 | tf_op jit(solution)/shard_map/ppermute | solution.py:195
  4.9 0.0 copy-done
  4.9 0.3 output_terms.1
  5.2 0.1 collective-permute-start.2
  5.3 0.5 %collective-permute-done.got = f32[2,2,40,128]{3,2,1,0:T(8,128)S(1)} collective-permute-done((f32[2,2,40,128]{3,2,1,0:T(8,128)S(1)}, f32[2,2,40,128]{3,2,1,0:T(8,128)S(1)}, u32[]{:S(2)}, u32[]{:S(2)}) %collective-permute-start) | collective-permute-done | bytes 81952 | tf_op jit(solution)/shard_map/ppermute | solution.py:195
  5.9 1.8 %collective-permute-start.1 = (f32[2,36,128]{2,1,0:T(8,128)S(1)}, f32[2,36,128]{2,1,0:T(8,128)S(1)}, u32[]{:S(2)}, u32[]{:S(2)}) collective-permute-start(f32[2,36,128]{2,1,0:T(8,128)S(1)} %get-tuple-element.19.after), channel_id=1, source_target_pairs={{0,96},{32,64},{64,32},{96,0},{1,97},{33,65},{65,33},{97,1},{2,98}... | collective-permute-start | bytes 110600 | tf_op jit(solution)/shard_map/ppermute | solution.py:195
  7.6 1.4 %collective-permute-done.2.got = f32[2,64,128]{2,1,0:T(8,128)S(1)} collective-permute-done((f32[2,64,128]{2,1,0:T(8,128)S(1)}, f32[2,64,128]{2,1,0:T(8,128)S(1)}, u32[]{:S(2)}, u32[]{:S(2)}) %collective-permute-start.2) | collective-permute-done | bytes 65568 | tf_op jit(solution)/shard_map/ppermute | solution.py:195
  9.1 0.8 %collective-permute-start.4 = (f32[64,128]{1,0:T(8,128)S(1)}, f32[64,128]{1,0:T(8,128)S(1)}, u32[]{:S(2)}, u32[]{:S(2)}) collective-permute-start(f32[64,128]{1,0:T(8,128)S(1)} %get-tuple-element.23.after), channel_id=1, source_target_pairs={{0,3},{1,2},{2,1},{3,0},{4,7},{5,6},{6,5},{7,4},{8,11},{9,10},{10,... | collective-permute-start | bytes 98312 | tf_op jit(solution)/shard_map/ppermute | solution.py:195
  9.9 0.1 collective-permute-done.1.got
  9.9 1.2 %collective-permute-start.3 = (f32[16,128]{1,0:T(8,128)S(1)}, f32[16,128]{1,0:T(8,128)S(1)}, u32[]{:S(2)}, u32[]{:S(2)}) collective-permute-start(f32[16,128]{1,0:T(8,128)S(1)} %get-tuple-element.25), channel_id=1, source_target_pairs={{0,32},{32,0},{64,96},{96,64},{1,33},{33,1},{65,97},{97,65},{2,34}... | collective-permute-start | bytes 24584 | tf_op jit(solution)/shard_map/ppermute | solution.py:195
  11.2 1.9 %collective-permute-done.4.out_got = f32[64,128]{1,0:T(8,128)S(1)} collective-permute-done((f32[64,128]{1,0:T(8,128)S(1)}, f32[64,128]{1,0:T(8,128)S(1)}, u32[]{:S(2)}, u32[]{:S(2)}) %collective-permute-start.4) | collective-permute-done | bytes 32800 | tf_op jit(solution)/shard_map/ppermute | solution.py:195
  13.1 0.0 collective-permute-done.3.in_got
  13.1 14.4 %all_to_all.10.packed = f32[8,40,128]{2,1,0:T(8,128)S(1)} all-to-all(f32[8,40,128]{2,1,0:T(8,128)S(1)} %pack_sides.1), channel_id=1, replica_groups=mesh['zh'=2,'y'=4,'core'=2,'zl'=4,'x'=4] {'zl','zh'}, dimensions={0} | all-to-all | bytes 327680 | tf_op jit(solution)/shard_map/all_to_all | solution.py:262
  27.5 0.2 feature_partials.1
  27.7 16.6 %all_to_all.11 = f32[32,2,128]{2,1,0:T(2,128)S(1)} all-to-all(f32[32,2,128]{2,1,0:T(2,128)S(1)} %bitcast.6), channel_id=1, replica_groups=mesh['zh'=2,'y'=4,'core'=2,'zl'=4,'x'=4] {'y','core','x'}, dimensions={0} | all-to-all | bytes 65536 | tf_op jit(solution)/shard_map/all_to_all | solution.py:271
  44.4 0.6 %reduce_sum.9 = f32[4,2,128]{2,1,0:T(2,128)} reduce(f32[8,4,2,128]{3,2,1,0:T(2,128)S(1)} %bitcast.8, f32[]{:T(128)} %constant.0.clone.1), dimensions={0}, to_apply=%region_0.0 | reduce | flops 7168 | bytes 36868 | tf_op jit(solution)/shard_map/reduce_sum | solution.py:274
  (4 shorter events, 0.0 us)
Async XLA Ops:
  0.0 4.9 %copy-start = (bf16[4,128,864]{1,2,0:T(8,128)(2,1)S(1)}, bf16[4,128,864]{1,2,0:T(8,128)(2,1)}, u32[]{:S(2)}) copy-start(bf16[4,128,864]{1,2,0:T(8,128)(2,1)} %param.5) | copy-start | bytes 2654212
  1.6 4.3 %collective-permute-start = (f32[2,2,40,128]{3,2,1,0:T(8,128)S(1)}, f32[2,2,40,128]{3,2,1,0:T(8,128)S(1)}, u32[]{:S(2)}, u32[]{:S(2)}) collective-permute-start(f32[2,2,40,128]{3,2,1,0:T(8,128)S(1)} %get-tuple-element.17), channel_id=1, source_target_pairs={{0,16},{16,0},{1,17},{17,1},{2,18},{18,2},{3,19},{19,3},{4,20},{20... | collective-permute-start | bytes 245768 | tf_op jit(solution)/shard_map/ppermute | solution.py:195
  5.2 3.8 %collective-permute-start.2 = (f32[2,64,128]{2,1,0:T(8,128)S(1)}, f32[2,64,128]{2,1,0:T(8,128)S(1)}, u32[]{:S(2)}, u32[]{:S(2)}) collective-permute-start(f32[2,64,128]{2,1,0:T(8,128)S(1)} %get-tuple-element.22), channel_id=1, source_target_pairs={{0,1},{1,0},{2,3},{3,2},{4,5},{5,4},{6,7},{7,6},{8,9},{9,8},{10,11... | collective-permute-start | bytes 196616 | tf_op jit(solution)/shard_map/ppermute | solution.py:195
  5.9 4.1 %collective-permute-start.1 = (f32[2,36,128]{2,1,0:T(8,128)S(1)}, f32[2,36,128]{2,1,0:T(8,128)S(1)}, u32[]{:S(2)}, u32[]{:S(2)}) collective-permute-start(f32[2,36,128]{2,1,0:T(8,128)S(1)} %get-tuple-element.19.after), channel_id=1, source_target_pairs={{0,96},{32,64},{64,32},{96,0},{1,97},{33,65},{65,33},{97,1},{2,98}... | collective-permute-start | bytes 110600 | tf_op jit(solution)/shard_map/ppermute | solution.py:195
  9.1 4.1 %collective-permute-start.4 = (f32[64,128]{1,0:T(8,128)S(1)}, f32[64,128]{1,0:T(8,128)S(1)}, u32[]{:S(2)}, u32[]{:S(2)}) collective-permute-start(f32[64,128]{1,0:T(8,128)S(1)} %get-tuple-element.23.after), channel_id=1, source_target_pairs={{0,3},{1,2},{2,1},{3,0},{4,7},{5,6},{6,5},{7,4},{8,11},{9,10},{10,... | collective-permute-start | bytes 98312 | tf_op jit(solution)/shard_map/ppermute | solution.py:195
  9.9 3.2 %collective-permute-start.3 = (f32[16,128]{1,0:T(8,128)S(1)}, f32[16,128]{1,0:T(8,128)S(1)}, u32[]{:S(2)}, u32[]{:S(2)}) collective-permute-start(f32[16,128]{1,0:T(8,128)S(1)} %get-tuple-element.25), channel_id=1, source_target_pairs={{0,32},{32,0},{64,96},{96,64},{1,33},{33,1},{65,97},{97,65},{2,34}... | collective-permute-start | bytes 24584 | tf_op jit(solution)/shard_map/ppermute | solution.py:195

commit v9 on v8

--- a/solution.py
+++ b/solution.py
@@ -21,10 +21,10 @@
 PART = SEQ_LEN // 2 // PARTS
 OUT_HERE = 32
 MULTIPLIER = 73244475
-AXES = ("zh", "y", "core", "zl", "x")
-SIZES = (2, 4, 2, 4, 4)
+AXES = ("zh", "y", "core", "za", "zb", "x")
+SIZES = (2, 4, 2, 2, 2, 4)
 ROW = ("zh", "y", "core")
-COL = ("zl", "x")
+COL = ("za", "zb", "x")
 
 SIN_TURN = (
     6.283185280154403,
@@ -66,7 +66,8 @@
 def input_kernel(
     seeds_hbm, offsets_hbm, acts, send, keep, out_table, seeds, offsets, held, blocks, arrived, told
 ):
-    zh, y, core, zl, x = (lax.axis_index(axis) for axis in AXES)
+    zh, y, core, za, zb, x = (lax.axis_index(axis) for axis in AXES)
+    zl = za * 2 + zb
     here = acts.shape[1]
     half = lax.shift_right_logical(zl, 1)
     tell = [
@@ -139,19 +140,19 @@
     for dest in range(8):
         half = (dest % 2) * OUT_HERE
         packed[dest, :OUT_HERE] = side_out[half : half + OUT_HERE]
-        half = (dest // 2 % 2) * IN_HERE
+        half = (dest // 4) * IN_HERE
         packed[dest, OUT_HERE:] = side_in[half : half + IN_HERE]
 
 
 def feature_kernel(packed, spread):
-    factor_half = lax.shift_right_logical(lax.axis_index("zl"), 1)
+    factor_half = lax.axis_index("za")
     sides_in, sides_out = [], []
     for z in range(2):
         sides_out.append(
             (packed[z, :OUT_HERE] + packed[2 + z, :OUT_HERE])
             + (packed[4 + z, :OUT_HERE] + packed[6 + z, :OUT_HERE])
         )
-        source = (z * 2 + factor_half) * 2
+        source = factor_half * 4 + z * 2
         sides_in.append(packed[source, OUT_HERE:] + packed[source + 1, OUT_HERE:])
     product = lax.dot_general(
         jnp.concatenate(sides_in, axis=1) * SEQ_LEN ** (-0.5),
@@ -164,7 +165,8 @@
         [product, jnp.zeros((IN_HERE, LANES - OUT_HERE), jnp.float32)], axis=1
     )
     for place in range(8):
-        spread[place] = total if place == 0 else pltpu.roll(total, LANES - 4 * place, 1)
+        moved = total if place == 0 else pltpu.roll(total, LANES - 4 * place, 1)
+        spread[place % 2 * 4 + place // 2] = moved
 
 
 def sum_kernel(parts, features):
@@ -259,7 +261,7 @@
         compiler_params=params,
         name="pack_sides",
     )(in_keep, in_got, out_keep, out_got)
-    packed = lax.all_to_all(packed, ("zl", "zh"), 0, 0, tiled=True)
+    packed = lax.all_to_all(packed, ("zb", "za", "zh"), 0, 0, tiled=True)
     spread = pl.pallas_call(
         feature_kernel,
         out_shape=shaped(8, 8, LANES),
@@ -269,7 +271,7 @@
         name="feature_partials",
     )(packed)
     spread = lax.all_to_all(
-        spread.reshape(32, 2, LANES), ("y", "core", "x"), 0, 0, tiled=True
+        spread.reshape(32, 2, LANES), ("core", "y", "x"), 0, 0, tiled=True
     )
     summed = jnp.sum(spread.reshape(8, SEQS, 2, LANES), axis=0)
     return summed[:, :, :4]

time: 45.2 us -> 44.7 us (0.989)
  blocking collectives: 31 us -> 30.5 us
    all_to_all x2, blocking collectives: 31 us -> 30.5 us  [the longest x1 16.2 us: body(): lax.all_to_all(spread.reshape(32, 2, LANES), ('core', 'y', 'x'), 0, 0, ti...]
where the time goes in v9:
time: 44.7 us; the launch traced here: 44.5 us
  blocking collectives  30.5 us (68%)
  starting transfers between devices  7.26 us (16%)
  waiting for transfers between devices  3.9 us (9%)
  Pallas kernels  2.15 us (5%)
  other arithmetic  0.62 us (1%)
    all_to_all x1, blocking collectives, body(): lax.all_to_all(spread.reshape(32, 2, LANES), ('core', 'y', 'x'), 0, 0, ti...  16.2 us
    all_to_all x1, blocking collectives, body(): packed = lax.all_to_all(packed, ('zb', 'za', 'zh'), 0, 0, tiled=True)  14.4 us
    ppermute x5, starting transfers between devices, swap(): return lax.ppermute(value, axis, [(i, i ^ distance) for i in range(size)])  7.26 us
    ppermute x5, waiting for transfers between devices, swap(): return lax.ppermute(value, axis, [(i, i ^ distance) for i in range(size)])  3.9 us
    pallas_call x1, Pallas kernels, body(): pl.pallas_call(input_kernel, out_shape=[shaped(2, 2, SENT_ROWS, LANES), s...  1.6 us
  transfers between devices with their start and end apart: 5, of which 4 were waited for; matrix products, arithmetic and copies ran while one was open for 0% of the time, Pallas kernels for 1%

profile of v9, /device:TPU:1, one launch (start us, length us, event | category | flops | bytes accessed | tf_op | source)
XLA Modules:
  0.0 44.5 jit_solution(1051479792861754816)
XLA Ops:
  0.0 0.0 copy-start
  0.0 1.6 %input_terms.1 = (f32[2,2,40,128]{3,2,1,0:T(8,128)S(1)}, f32[2,2,16,128]{3,2,1,0:T(8,128)S(1)}, bf16[64,864]{1,0:T(8,128)(2,1)S(1)}) custom-call(s32[2]{0:T(128)} %seeds_hbm.1, s32[2]{0:T(128)} %offsets_hbm.1, bf16[4,320,2048]{2,1,0:T(8,128)(2,1)} %bitcast.7), custom_call_target="tpu_custom_call" | custom-call | tf_op jit(solution)/shard_map/input_terms/pallas_call | solution.py:209
  1.6 3.3 %collective-permute-start = (f32[2,2,40,128]{3,2,1,0:T(8,128)S(1)}, f32[2,2,40,128]{3,2,1,0:T(8,128)S(1)}, u32[]{:S(2)}, u32[]{:S(2)}) collective-permute-start(f32[2,2,40,128]{3,2,1,0:T(8,128)S(1)} %get-tuple-element.17), channel_id=1, source_target_pairs={{0,16},{16,0},{1,17},{17,1},{2,18},{18,2},{3,19},{19,3},{4,20},{20... | collective-permute-start | bytes 245768 | tf_op jit(solution)/shard_map/ppermute | solution.py:197
  4.9 0.0 copy-done
  4.9 0.3 output_terms.1
  5.2 0.1 collective-permute-start.2
  5.3 0.5 %collective-permute-done.got = f32[2,2,40,128]{3,2,1,0:T(8,128)S(1)} collective-permute-done((f32[2,2,40,128]{3,2,1,0:T(8,128)S(1)}, f32[2,2,40,128]{3,2,1,0:T(8,128)S(1)}, u32[]{:S(2)}, u32[]{:S(2)}) %collective-permute-start) | collective-permute-done | bytes 81952 | tf_op jit(solution)/shard_map/ppermute | solution.py:197
  5.9 1.8 %collective-permute-start.1 = (f32[2,36,128]{2,1,0:T(8,128)S(1)}, f32[2,36,128]{2,1,0:T(8,128)S(1)}, u32[]{:S(2)}, u32[]{:S(2)}) collective-permute-start(f32[2,36,128]{2,1,0:T(8,128)S(1)} %get-tuple-element.19.after), channel_id=1, source_target_pairs={{0,96},{32,64},{64,32},{96,0},{1,97},{33,65},{65,33},{97,1},{2,98}... | collective-permute-start | bytes 110600 | tf_op jit(solution)/shard_map/ppermute | solution.py:197
  7.6 1.4 %collective-permute-done.2.got = f32[2,64,128]{2,1,0:T(8,128)S(1)} collective-permute-done((f32[2,64,128]{2,1,0:T(8,128)S(1)}, f32[2,64,128]{2,1,0:T(8,128)S(1)}, u32[]{:S(2)}, u32[]{:S(2)}) %collective-permute-start.2) | collective-permute-done | bytes 65568 | tf_op jit(solution)/shard_map/ppermute | solution.py:197
  9.1 0.8 %collective-permute-start.4 = (f32[64,128]{1,0:T(8,128)S(1)}, f32[64,128]{1,0:T(8,128)S(1)}, u32[]{:S(2)}, u32[]{:S(2)}) collective-permute-start(f32[64,128]{1,0:T(8,128)S(1)} %get-tuple-element.23.after), channel_id=1, source_target_pairs={{0,3},{1,2},{2,1},{3,0},{4,7},{5,6},{6,5},{7,4},{8,11},{9,10},{10,... | collective-permute-start | bytes 98312 | tf_op jit(solution)/shard_map/ppermute | solution.py:197
  9.9 0.1 collective-permute-done.1.got
  9.9 1.2 %collective-permute-start.3 = (f32[16,128]{1,0:T(8,128)S(1)}, f32[16,128]{1,0:T(8,128)S(1)}, u32[]{:S(2)}, u32[]{:S(2)}) collective-permute-start(f32[16,128]{1,0:T(8,128)S(1)} %get-tuple-element.25), channel_id=1, source_target_pairs={{0,32},{32,0},{64,96},{96,64},{1,33},{33,1},{65,97},{97,65},{2,34}... | collective-permute-start | bytes 24584 | tf_op jit(solution)/shard_map/ppermute | solution.py:197
  11.2 1.9 %collective-permute-done.4.out_got = f32[64,128]{1,0:T(8,128)S(1)} collective-permute-done((f32[64,128]{1,0:T(8,128)S(1)}, f32[64,128]{1,0:T(8,128)S(1)}, u32[]{:S(2)}, u32[]{:S(2)}) %collective-permute-start.4) | collective-permute-done | bytes 32800 | tf_op jit(solution)/shard_map/ppermute | solution.py:197
  13.1 0.0 collective-permute-done.3.in_got
  13.1 14.4 %all_to_all.10.packed = f32[8,40,128]{2,1,0:T(8,128)S(1)} all-to-all(f32[8,40,128]{2,1,0:T(8,128)S(1)} %pack_sides.1), channel_id=1, replica_groups=mesh['zh'=2,'y'=4,'core'=2,'za'=2,'zb'=2,'x'=4] {'zb','za','zh'}, dimensions={0} | all-to-all | bytes 327680 | tf_op jit(solution)/shard_map/all_to_all | solution.py:264
  27.5 0.2 feature_partials.1
  27.7 16.2 %all_to_all.11 = f32[32,2,128]{2,1,0:T(2,128)S(1)} all-to-all(f32[32,2,128]{2,1,0:T(2,128)S(1)} %bitcast.6), channel_id=1, replica_groups=mesh['zh'=2,'y'=4,'core'=2,'za'=2,'zb'=2,'x'=4] {'core','y','x'}, dimensions={0} | all-to-all | bytes 65536 | tf_op jit(solution)/shard_map/all_to_all | solution.py:273
  43.9 0.6 %reduce_sum.9 = f32[4,2,128]{2,1,0:T(2,128)} reduce(f32[8,4,2,128]{3,2,1,0:T(2,128)S(1)} %bitcast.8, f32[]{:T(128)} %constant.0.clone.1), dimensions={0}, to_apply=%region_0.0 | reduce | flops 7168 | bytes 36868 | tf_op jit(solution)/shard_map/reduce_sum | solution.py:276
  (4 shorter events, 0.0 us)
Async XLA Ops:
  0.0 4.9 %copy-start = (bf16[4,128,864]{1,2,0:T(8,128)(2,1)S(1)}, bf16[4,128,864]{1,2,0:T(8,128)(2,1)}, u32[]{:S(2)}) copy-start(bf16[4,128,864]{1,2,0:T(8,128)(2,1)} %param.5) | copy-start | bytes 2654212
  1.6 4.3 %collective-permute-start = (f32[2,2,40,128]{3,2,1,0:T(8,128)S(1)}, f32[2,2,40,128]{3,2,1,0:T(8,128)S(1)}, u32[]{:S(2)}, u32[]{:S(2)}) collective-permute-start(f32[2,2,40,128]{3,2,1,0:T(8,128)S(1)} %get-tuple-element.17), channel_id=1, source_target_pairs={{0,16},{16,0},{1,17},{17,1},{2,18},{18,2},{3,19},{19,3},{4,20},{20... | collective-permute-start | bytes 245768 | tf_op jit(solution)/shard_map/ppermute | solution.py:197
  5.2 3.8 %collective-permute-start.2 = (f32[2,64,128]{2,1,0:T(8,128)S(1)}, f32[2,64,128]{2,1,0:T(8,128)S(1)}, u32[]{:S(2)}, u32[]{:S(2)}) collective-permute-start(f32[2,64,128]{2,1,0:T(8,128)S(1)} %get-tuple-element.22), channel_id=1, source_target_pairs={{0,1},{1,0},{2,3},{3,2},{4,5},{5,4},{6,7},{7,6},{8,9},{9,8},{10,11... | collective-permute-start | bytes 196616 | tf_op jit(solution)/shard_map/ppermute | solution.py:197
  5.9 4.1 %collective-permute-start.1 = (f32[2,36,128]{2,1,0:T(8,128)S(1)}, f32[2,36,128]{2,1,0:T(8,128)S(1)}, u32[]{:S(2)}, u32[]{:S(2)}) collective-permute-start(f32[2,36,128]{2,1,0:T(8,128)S(1)} %get-tuple-element.19.after), channel_id=1, source_target_pairs={{0,96},{32,64},{64,32},{96,0},{1,97},{33,65},{65,33},{97,1},{2,98}... | collective-permute-start | bytes 110600 | tf_op jit(solution)/shard_map/ppermute | solution.py:197
  9.1 4.1 %collective-permute-start.4 = (f32[64,128]{1,0:T(8,128)S(1)}, f32[64,128]{1,0:T(8,128)S(1)}, u32[]{:S(2)}, u32[]{:S(2)}) collective-permute-start(f32[64,128]{1,0:T(8,128)S(1)} %get-tuple-element.23.after), channel_id=1, source_target_pairs={{0,3},{1,2},{2,1},{3,0},{4,7},{5,6},{6,5},{7,4},{8,11},{9,10},{10,... | collective-permute-start | bytes 98312 | tf_op jit(solution)/shard_map/ppermute | solution.py:197
  9.9 3.2 %collective-permute-start.3 = (f32[16,128]{1,0:T(8,128)S(1)}, f32[16,128]{1,0:T(8,128)S(1)}, u32[]{:S(2)}, u32[]{:S(2)}) collective-permute-start(f32[16,128]{1,0:T(8,128)S(1)} %get-tuple-element.25), channel_id=1, source_target_pairs={{0,32},{32,0},{64,96},{96,64},{1,33},{33,1},{65,97},{97,65},{2,34}... | collective-permute-start | bytes 24584 | tf_op jit(solution)/shard_map/ppermute | solution.py:197

commit v10 on v9

--- a/solution.py
+++ b/solution.py
@@ -17,7 +17,7 @@
 IN_SENT = 16
 SENT_ROWS = 40
 PADDED_ROWS = 36
-PARTS = 2
+PARTS = 1
 PART = SEQ_LEN // 2 // PARTS
 OUT_HERE = 32
 MULTIPLIER = 73244475

time: 44.7 us -> 44.6 us (level)
  transfers between devices with their start and end apart: 5 -> 5, of which waited for: 4 -> 3; matrix products, arithmetic and copies ran while one was open for 0% -> 0% of each run, Pallas kernels for 1% -> 1%
where the time goes in v10:
time: 44.6 us; the launch traced here: 44.4 us
  blocking collectives  30.5 us (68%)
  starting transfers between devices  7.27 us (16%)
  waiting for transfers between devices  3.89 us (9%)
  Pallas kernels  2.03 us (5%)
  other arithmetic  0.62 us (1%)
    all_to_all x1, blocking collectives, body(): lax.all_to_all(spread.reshape(32, 2, LANES), ('core', 'y', 'x'), 0, 0, ti...  16.2 us
    all_to_all x1, blocking collectives, body(): packed = lax.all_to_all(packed, ('zb', 'za', 'zh'), 0, 0, tiled=True)  14.4 us
    ppermute x5, starting transfers between devices, swap(): return lax.ppermute(value, axis, [(i, i ^ distance) for i in range(size)])  7.27 us
    ppermute x5, waiting for transfers between devices, swap(): return lax.ppermute(value, axis, [(i, i ^ distance) for i in range(size)])  3.89 us
    pallas_call x1, Pallas kernels, body(): pl.pallas_call(input_kernel, out_shape=[shaped(2, 2, SENT_ROWS, LANES), s...  1.49 us
  transfers between devices with their start and end apart: 5, of which 3 were waited for; matrix products, arithmetic and copies ran while one was open for 0% of the time, Pallas kernels for 1%

profile of v10, /device:TPU:1, one launch (start us, length us, event | category | flops | bytes accessed | tf_op | source)
XLA Modules:
  0.0 44.4 jit_solution(15258805507753924242)
XLA Ops:
  0.0 0.0 copy-start
  0.0 1.5 %input_terms.1 = (f32[2,2,40,128]{3,2,1,0:T(8,128)S(1)}, f32[2,2,16,128]{3,2,1,0:T(8,128)S(1)}, bf16[64,864]{1,0:T(8,128)(2,1)S(1)}) custom-call(s32[2]{0:T(128)} %seeds_hbm.1, s32[2]{0:T(128)} %offsets_hbm.1, bf16[4,320,2048]{2,1,0:T(8,128)(2,1)} %bitcast.7), custom_call_target="tpu_custom_call" | custom-call | tf_op jit(solution)/shard_map/input_terms/pallas_call | solution.py:209
  1.5 3.3 %collective-permute-start = (f32[2,2,40,128]{3,2,1,0:T(8,128)S(1)}, f32[2,2,40,128]{3,2,1,0:T(8,128)S(1)}, u32[]{:S(2)}, u32[]{:S(2)}) collective-permute-start(f32[2,2,40,128]{3,2,1,0:T(8,128)S(1)} %get-tuple-element.17), channel_id=1, source_target_pairs={{0,16},{16,0},{1,17},{17,1},{2,18},{18,2},{3,19},{19,3},{4,20},{20... | collective-permute-start | bytes 245768 | tf_op jit(solution)/shard_map/ppermute | solution.py:197
  4.8 0.0 copy-done
  4.8 0.3 output_terms.1
  5.1 0.1 collective-permute-start.2
  5.2 0.5 %collective-permute-done.got = f32[2,2,40,128]{3,2,1,0:T(8,128)S(1)} collective-permute-done((f32[2,2,40,128]{3,2,1,0:T(8,128)S(1)}, f32[2,2,40,128]{3,2,1,0:T(8,128)S(1)}, u32[]{:S(2)}, u32[]{:S(2)}) %collective-permute-start) | collective-permute-done | bytes 81952 | tf_op jit(solution)/shard_map/ppermute | solution.py:197
  5.8 1.8 %collective-permute-start.1 = (f32[2,36,128]{2,1,0:T(8,128)S(1)}, f32[2,36,128]{2,1,0:T(8,128)S(1)}, u32[]{:S(2)}, u32[]{:S(2)}) collective-permute-start(f32[2,36,128]{2,1,0:T(8,128)S(1)} %get-tuple-element.19.after), channel_id=1, source_target_pairs={{0,96},{32,64},{64,32},{96,0},{1,97},{33,65},{65,33},{97,1},{2,98}... | collective-permute-start | bytes 110600 | tf_op jit(solution)/shard_map/ppermute | solution.py:197
  7.5 1.4 %collective-permute-done.2.got = f32[2,64,128]{2,1,0:T(8,128)S(1)} collective-permute-done((f32[2,64,128]{2,1,0:T(8,128)S(1)}, f32[2,64,128]{2,1,0:T(8,128)S(1)}, u32[]{:S(2)}, u32[]{:S(2)}) %collective-permute-start.2) | collective-permute-done | bytes 65568 | tf_op jit(solution)/shard_map/ppermute | solution.py:197
  8.9 0.8 %collective-permute-start.4 = (f32[64,128]{1,0:T(8,128)S(1)}, f32[64,128]{1,0:T(8,128)S(1)}, u32[]{:S(2)}, u32[]{:S(2)}) collective-permute-start(f32[64,128]{1,0:T(8,128)S(1)} %get-tuple-element.23.after), channel_id=1, source_target_pairs={{0,3},{1,2},{2,1},{3,0},{4,7},{5,6},{6,5},{7,4},{8,11},{9,10},{10,... | collective-permute-start | bytes 98312 | tf_op jit(solution)/shard_map/ppermute | solution.py:197
  9.8 0.0 collective-permute-done.1.got
  9.8 1.2 %collective-permute-start.3 = (f32[16,128]{1,0:T(8,128)S(1)}, f32[16,128]{1,0:T(8,128)S(1)}, u32[]{:S(2)}, u32[]{:S(2)}) collective-permute-start(f32[16,128]{1,0:T(8,128)S(1)} %get-tuple-element.25), channel_id=1, source_target_pairs={{0,32},{32,0},{64,96},{96,64},{1,33},{33,1},{65,97},{97,65},{2,34}... | collective-permute-start | bytes 24584 | tf_op jit(solution)/shard_map/ppermute | solution.py:197
  11.1 1.9 %collective-permute-done.4.out_got = f32[64,128]{1,0:T(8,128)S(1)} collective-permute-done((f32[64,128]{1,0:T(8,128)S(1)}, f32[64,128]{1,0:T(8,128)S(1)}, u32[]{:S(2)}, u32[]{:S(2)}) %collective-permute-start.4) | collective-permute-done | bytes 32800 | tf_op jit(solution)/shard_map/ppermute | solution.py:197
  13.0 0.0 collective-permute-done.3.in_got
  13.0 14.4 %all_to_all.10.packed = f32[8,40,128]{2,1,0:T(8,128)S(1)} all-to-all(f32[8,40,128]{2,1,0:T(8,128)S(1)} %pack_sides.1), channel_id=1, replica_groups=mesh['zh'=2,'y'=4,'core'=2,'za'=2,'zb'=2,'x'=4] {'zb','za','zh'}, dimensions={0} | all-to-all | bytes 327680 | tf_op jit(solution)/shard_map/all_to_all | solution.py:264
  27.4 0.2 feature_partials.1
  27.6 16.2 %all_to_all.11 = f32[32,2,128]{2,1,0:T(2,128)S(1)} all-to-all(f32[32,2,128]{2,1,0:T(2,128)S(1)} %bitcast.6), channel_id=1, replica_groups=mesh['zh'=2,'y'=4,'core'=2,'za'=2,'zb'=2,'x'=4] {'core','y','x'}, dimensions={0} | all-to-all | bytes 65536 | tf_op jit(solution)/shard_map/all_to_all | solution.py:273
  43.8 0.6 %reduce_sum.9 = f32[4,2,128]{2,1,0:T(2,128)} reduce(f32[8,4,2,128]{3,2,1,0:T(2,128)S(1)} %bitcast.8, f32[]{:T(128)} %constant.0.clone.1), dimensions={0}, to_apply=%region_0.0 | reduce | flops 7168 | bytes 36868 | tf_op jit(solution)/shard_map/reduce_sum | solution.py:276
  (4 shorter events, 0.0 us)
Async XLA Ops:
  0.0 4.8 %copy-start = (bf16[4,128,864]{1,2,0:T(8,128)(2,1)S(1)}, bf16[4,128,864]{1,2,0:T(8,128)(2,1)}, u32[]{:S(2)}) copy-start(bf16[4,128,864]{1,2,0:T(8,128)(2,1)} %param.5) | copy-start | bytes 2654212
  1.5 4.3 %collective-permute-start = (f32[2,2,40,128]{3,2,1,0:T(8,128)S(1)}, f32[2,2,40,128]{3,2,1,0:T(8,128)S(1)}, u32[]{:S(2)}, u32[]{:S(2)}) collective-permute-start(f32[2,2,40,128]{3,2,1,0:T(8,128)S(1)} %get-tuple-element.17), channel_id=1, source_target_pairs={{0,16},{16,0},{1,17},{17,1},{2,18},{18,2},{3,19},{19,3},{4,20},{20... | collective-permute-start | bytes 245768 | tf_op jit(solution)/shard_map/ppermute | solution.py:197
  5.1 3.8 %collective-permute-start.2 = (f32[2,64,128]{2,1,0:T(8,128)S(1)}, f32[2,64,128]{2,1,0:T(8,128)S(1)}, u32[]{:S(2)}, u32[]{:S(2)}) collective-permute-start(f32[2,64,128]{2,1,0:T(8,128)S(1)} %get-tuple-element.22), channel_id=1, source_target_pairs={{0,1},{1,0},{2,3},{3,2},{4,5},{5,4},{6,7},{7,6},{8,9},{9,8},{10,11... | collective-permute-start | bytes 196616 | tf_op jit(solution)/shard_map/ppermute | solution.py:197
  5.8 4.1 %collective-permute-start.1 = (f32[2,36,128]{2,1,0:T(8,128)S(1)}, f32[2,36,128]{2,1,0:T(8,128)S(1)}, u32[]{:S(2)}, u32[]{:S(2)}) collective-permute-start(f32[2,36,128]{2,1,0:T(8,128)S(1)} %get-tuple-element.19.after), channel_id=1, source_target_pairs={{0,96},{32,64},{64,32},{96,0},{1,97},{33,65},{65,33},{97,1},{2,98}... | collective-permute-start | bytes 110600 | tf_op jit(solution)/shard_map/ppermute | solution.py:197
  8.9 4.1 %collective-permute-start.4 = (f32[64,128]{1,0:T(8,128)S(1)}, f32[64,128]{1,0:T(8,128)S(1)}, u32[]{:S(2)}, u32[]{:S(2)}) collective-permute-start(f32[64,128]{1,0:T(8,128)S(1)} %get-tuple-element.23.after), channel_id=1, source_target_pairs={{0,3},{1,2},{2,1},{3,0},{4,7},{5,6},{6,5},{7,4},{8,11},{9,10},{10,... | collective-permute-start | bytes 98312 | tf_op jit(solution)/shard_map/ppermute | solution.py:197
  9.8 3.2 %collective-permute-start.3 = (f32[16,128]{1,0:T(8,128)S(1)}, f32[16,128]{1,0:T(8,128)S(1)}, u32[]{:S(2)}, u32[]{:S(2)}) collective-permute-start(f32[16,128]{1,0:T(8,128)S(1)} %get-tuple-element.25), channel_id=1, source_target_pairs={{0,32},{32,0},{64,96},{96,64},{1,33},{33,1},{65,97},{97,65},{2,34}... | collective-permute-start | bytes 24584 | tf_op jit(solution)/shard_map/ppermute | solution.py:197

commit v11 on v10

--- a/solution.py
+++ b/solution.py
@@ -15,8 +15,8 @@
 BLOCKS = SEQ_LEN // LANES
 IN_HERE = 8
 IN_SENT = 16
-SENT_ROWS = 40
-PADDED_ROWS = 36
+SENT_ROWS = 36
+PADDED_ROWS = 33
 PARTS = 1
 PART = SEQ_LEN // 2 // PARTS
 OUT_HERE = 32

time: 44.6 us -> 44.6 us (level)
  no operation moved by 1% of the time
where the time goes in v11:
time: 44.6 us; the launch traced here: 44.4 us
  blocking collectives  30.5 us (68%)
  starting transfers between devices  7.27 us (16%)
  waiting for transfers between devices  3.89 us (9%)
  Pallas kernels  2.03 us (5%)
  other arithmetic  0.62 us (1%)
    all_to_all x1, blocking collectives, body(): lax.all_to_all(spread.reshape(32, 2, LANES), ('core', 'y', 'x'), 0, 0, ti...  16.2 us
    all_to_all x1, blocking collectives, body(): packed = lax.all_to_all(packed, ('zb', 'za', 'zh'), 0, 0, tiled=True)  14.4 us
    ppermute x5, starting transfers between devices, swap(): return lax.ppermute(value, axis, [(i, i ^ distance) for i in range(size)])  7.27 us
    ppermute x5, waiting for transfers between devices, swap(): return lax.ppermute(value, axis, [(i, i ^ distance) for i in range(size)])  3.89 us
    pallas_call x1, Pallas kernels, body(): pl.pallas_call(input_kernel, out_shape=[shaped(2, 2, SENT_ROWS, LANES), s...  1.49 us
  transfers between devices with their start and end apart: 5, of which 3 were waited for; matrix products, arithmetic and copies ran while one was open for 0% of the time, Pallas kernels for 1%

profile of v11, /device:TPU:1, one launch (start us, length us, event | category | flops | bytes accessed | tf_op | source)
XLA Modules:
  0.0 44.4 jit_solution(16712338912441560249)
XLA Ops:
  0.0 0.0 copy-start
  0.0 1.5 %input_terms.1 = (f32[2,2,36,128]{3,2,1,0:T(8,128)S(1)}, f32[2,2,16,128]{3,2,1,0:T(8,128)S(1)}, bf16[64,864]{1,0:T(8,128)(2,1)S(1)}) custom-call(s32[2]{0:T(128)} %seeds_hbm.1, s32[2]{0:T(128)} %offsets_hbm.1, bf16[4,320,2048]{2,1,0:T(8,128)(2,1)} %bitcast.7), custom_call_target="tpu_custom_call" | custom-call | tf_op jit(solution)/shard_map/input_terms/pallas_call | solution.py:209
  1.5 3.3 %collective-permute-start = (f32[2,2,36,128]{3,2,1,0:T(8,128)S(1)}, f32[2,2,36,128]{3,2,1,0:T(8,128)S(1)}, u32[]{:S(2)}, u32[]{:S(2)}) collective-permute-start(f32[2,2,36,128]{3,2,1,0:T(8,128)S(1)} %get-tuple-element.17), channel_id=1, source_target_pairs={{0,16},{16,0},{1,17},{17,1},{2,18},{18,2},{3,19},{19,3},{4,20},{20... | collective-permute-start | bytes 221192 | tf_op jit(solution)/shard_map/ppermute | solution.py:197
  4.8 0.0 copy-done
  4.8 0.3 output_terms.1
  5.1 0.1 collective-permute-start.2
  5.2 0.5 %collective-permute-done.got = f32[2,2,36,128]{3,2,1,0:T(8,128)S(1)} collective-permute-done((f32[2,2,36,128]{3,2,1,0:T(8,128)S(1)}, f32[2,2,36,128]{3,2,1,0:T(8,128)S(1)}, u32[]{:S(2)}, u32[]{:S(2)}) %collective-permute-start) | collective-permute-done | bytes 73760 | tf_op jit(solution)/shard_map/ppermute | solution.py:197
  5.8 1.8 %collective-permute-start.1 = (f32[2,33,128]{2,1,0:T(8,128)S(1)}, f32[2,33,128]{2,1,0:T(8,128)S(1)}, u32[]{:S(2)}, u32[]{:S(2)}) collective-permute-start(f32[2,33,128]{2,1,0:T(8,128)S(1)} %get-tuple-element.19.after), channel_id=1, source_target_pairs={{0,96},{32,64},{64,32},{96,0},{1,97},{33,65},{65,33},{97,1},{2,98}... | collective-permute-start | bytes 101384 | tf_op jit(solution)/shard_map/ppermute | solution.py:197
  7.5 1.4 %collective-permute-done.2.got = f32[2,64,128]{2,1,0:T(8,128)S(1)} collective-permute-done((f32[2,64,128]{2,1,0:T(8,128)S(1)}, f32[2,64,128]{2,1,0:T(8,128)S(1)}, u32[]{:S(2)}, u32[]{:S(2)}) %collective-permute-start.2) | collective-permute-done | bytes 65568 | tf_op jit(solution)/shard_map/ppermute | solution.py:197
  8.9 0.8 %collective-permute-start.4 = (f32[64,128]{1,0:T(8,128)S(1)}, f32[64,128]{1,0:T(8,128)S(1)}, u32[]{:S(2)}, u32[]{:S(2)}) collective-permute-start(f32[64,128]{1,0:T(8,128)S(1)} %get-tuple-element.23.after), channel_id=1, source_target_pairs={{0,3},{1,2},{2,1},{3,0},{4,7},{5,6},{6,5},{7,4},{8,11},{9,10},{10,... | collective-permute-start | bytes 98312 | tf_op jit(solution)/shard_map/ppermute | solution.py:197
  9.8 0.0 collective-permute-done.1.got
  9.8 1.2 %collective-permute-start.3 = (f32[16,128]{1,0:T(8,128)S(1)}, f32[16,128]{1,0:T(8,128)S(1)}, u32[]{:S(2)}, u32[]{:S(2)}) collective-permute-start(f32[16,128]{1,0:T(8,128)S(1)} %get-tuple-element.25), channel_id=1, source_target_pairs={{0,32},{32,0},{64,96},{96,64},{1,33},{33,1},{65,97},{97,65},{2,34}... | collective-permute-start | bytes 24584 | tf_op jit(solution)/shard_map/ppermute | solution.py:197
  11.1 1.9 %collective-permute-done.4.out_got = f32[64,128]{1,0:T(8,128)S(1)} collective-permute-done((f32[64,128]{1,0:T(8,128)S(1)}, f32[64,128]{1,0:T(8,128)S(1)}, u32[]{:S(2)}, u32[]{:S(2)}) %collective-permute-start.4) | collective-permute-done | bytes 32800 | tf_op jit(solution)/shard_map/ppermute | solution.py:197
  13.0 0.0 collective-permute-done.3.in_got
  13.0 14.4 %all_to_all.10.packed = f32[8,40,128]{2,1,0:T(8,128)S(1)} all-to-all(f32[8,40,128]{2,1,0:T(8,128)S(1)} %pack_sides.1), channel_id=1, replica_groups=mesh['zh'=2,'y'=4,'core'=2,'za'=2,'zb'=2,'x'=4] {'zb','za','zh'}, dimensions={0} | all-to-all | bytes 327680 | tf_op jit(solution)/shard_map/all_to_all | solution.py:264
  27.4 0.2 feature_partials.1
  27.6 16.2 %all_to_all.11 = f32[32,2,128]{2,1,0:T(2,128)S(1)} all-to-all(f32[32,2,128]{2,1,0:T(2,128)S(1)} %bitcast.6), channel_id=1, replica_groups=mesh['zh'=2,'y'=4,'core'=2,'za'=2,'zb'=2,'x'=4] {'core','y','x'}, dimensions={0} | all-to-all | bytes 65536 | tf_op jit(solution)/shard_map/all_to_all | solution.py:273
  43.8 0.6 %reduce_sum.9 = f32[4,2,128]{2,1,0:T(2,128)} reduce(f32[8,4,2,128]{3,2,1,0:T(2,128)S(1)} %bitcast.8, f32[]{:T(128)} %constant.0.clone.1), dimensions={0}, to_apply=%region_0.0 | reduce | flops 7168 | bytes 36868 | tf_op jit(solution)/shard_map/reduce_sum | solution.py:276
  (4 shorter events, 0.0 us)
Async XLA Ops:
  0.0 4.8 %copy-start = (bf16[4,128,864]{1,2,0:T(8,128)(2,1)S(1)}, bf16[4,128,864]{1,2,0:T(8,128)(2,1)}, u32[]{:S(2)}) copy-start(bf16[4,128,864]{1,2,0:T(8,128)(2,1)} %param.5) | copy-start | bytes 2654212
  1.5 4.3 %collective-permute-start = (f32[2,2,36,128]{3,2,1,0:T(8,128)S(1)}, f32[2,2,36,128]{3,2,1,0:T(8,128)S(1)}, u32[]{:S(2)}, u32[]{:S(2)}) collective-permute-start(f32[2,2,36,128]{3,2,1,0:T(8,128)S(1)} %get-tuple-element.17), channel_id=1, source_target_pairs={{0,16},{16,0},{1,17},{17,1},{2,18},{18,2},{3,19},{19,3},{4,20},{20... | collective-permute-start | bytes 221192 | tf_op jit(solution)/shard_map/ppermute | solution.py:197
  5.1 3.8 %collective-permute-start.2 = (f32[2,64,128]{2,1,0:T(8,128)S(1)}, f32[2,64,128]{2,1,0:T(8,128)S(1)}, u32[]{:S(2)}, u32[]{:S(2)}) collective-permute-start(f32[2,64,128]{2,1,0:T(8,128)S(1)} %get-tuple-element.22), channel_id=1, source_target_pairs={{0,1},{1,0},{2,3},{3,2},{4,5},{5,4},{6,7},{7,6},{8,9},{9,8},{10,11... | collective-permute-start | bytes 196616 | tf_op jit(solution)/shard_map/ppermute | solution.py:197
  5.8 4.1 %collective-permute-start.1 = (f32[2,33,128]{2,1,0:T(8,128)S(1)}, f32[2,33,128]{2,1,0:T(8,128)S(1)}, u32[]{:S(2)}, u32[]{:S(2)}) collective-permute-start(f32[2,33,128]{2,1,0:T(8,128)S(1)} %get-tuple-element.19.after), channel_id=1, source_target_pairs={{0,96},{32,64},{64,32},{96,0},{1,97},{33,65},{65,33},{97,1},{2,98}... | collective-permute-start | bytes 101384 | tf_op jit(solution)/shard_map/ppermute | solution.py:197
  8.9 4.1 %collective-permute-start.4 = (f32[64,128]{1,0:T(8,128)S(1)}, f32[64,128]{1,0:T(8,128)S(1)}, u32[]{:S(2)}, u32[]{:S(2)}) collective-permute-start(f32[64,128]{1,0:T(8,128)S(1)} %get-tuple-element.23.after), channel_id=1, source_target_pairs={{0,3},{1,2},{2,1},{3,0},{4,7},{5,6},{6,5},{7,4},{8,11},{9,10},{10,... | collective-permute-start | bytes 98312 | tf_op jit(solution)/shard_map/ppermute | solution.py:197
  9.8 3.2 %collective-permute-start.3 = (f32[16,128]{1,0:T(8,128)S(1)}, f32[16,128]{1,0:T(8,128)S(1)}, u32[]{:S(2)}, u32[]{:S(2)}) collective-permute-start(f32[16,128]{1,0:T(8,128)S(1)} %get-tuple-element.25), channel_id=1, source_target_pairs={{0,32},{32,0},{64,96},{96,64},{1,33},{33,1},{65,97},{97,65},{2,34}... | collective-permute-start | bytes 24584 | tf_op jit(solution)/shard_map/ppermute | solution.py:197
